TPU v7x, 1024 devices: a whole 8x8x8 slice. The times are simulated.
1024 devices in a mesh: row: 64 (over z, x), col: 16 (over y, core).
Axes of the slice: x: 8, y: 8, z: 8, core: 2. Of those that a mesh axis runs over, the one named last changes fastest.
Arguments:
- features: bfloat16 [524288, 256], P(('row', 'col')), may hold values from -6 to 6
- w_self: bfloat16 [256, 256], replicated, may hold values from -0.375 to 0.375
- w_neigh: bfloat16 [256, 256], replicated, may hold values from -0.375 to 0.375
- local_weight: bfloat16 [524288, 512], P(('row', 'col')), as said below
- hub_rows: int32 [1024, 1], P(('row', 'col')), may hold values from 0 to 511
- hub_weight: bfloat16 [524288, 1024], P(('row', 'col')), as said below
- send_rows: int32 [1024, 16, 16], P(('row', 'col')), may hold values from 0 to 511
- send_count: int32 [1024, 16], P(('row', 'col')), may hold values from 1 to 16, as said below
- halo_weight: bfloat16 [524288, 256], P(('row', 'col')), as said below
- grad_out: bfloat16 [524288, 256], P(('row', 'col')), may hold values from -6 to 6
Outputs:
- output: bfloat16 [524288, 256], P(('row', 'col'))
- grad_features: bfloat16 [524288, 256], P(('row', 'col'))
- grad_self: float32 [256, 256], replicated
- grad_neigh: float32 [256, 256], replicated
Inputs may be any that keep to these rules, and one draw needn't show every extreme that they name: `local_weight`: A weight is zero where there is no edge and positive where there is one. `hub_weight`: A weight is zero where there is no edge and positive where there is one. `halo_weight`: A weight is zero where there is no edge and positive where there is one. `hub_rows`: rows within the owning part's block. `send_rows`: rows within the sending part's block; only the first send_count of each list are sent. `send_count`: in every group of a row index some part receives 16 rows from every part of its group.
All inputs are finite; a program needn't handle non-finite values.
Results may differ from a plain program's by a relative error of at most 0.0051.
Values may be sent and summed in bfloat16 or wider, within the bound.
No kernel may reach another device: no remote copies, remote signals or barrier semaphores. Data moves between devices by JAX's collectives and lax.ppermute only.
A program may use at most 32 MiB of HBM per device.

v0:
```python
import jax
import jax.numpy as jnp
from jax import lax
from jax.sharding import PartitionSpec as P


def per_device(
    features,
    w_self,
    w_neigh,
    local_weight,
    hub_rows,
    hub_weight,
    send_rows,
    send_count,
    halo_weight,
    grad_out,
):
    node_count, feat_width = features.shape
    peer_count = send_rows.shape[1]
    slot_count = send_rows.shape[2]
    hub_local = features[hub_rows[0]]
    send_index = send_rows[0].reshape(-1)
    send_buffer = features[send_index].reshape(peer_count, slot_count, feat_width)
    arrived, arrived_count = (
        lax.all_to_all(send_buffer, "col", split_axis=0, concat_axis=0, tiled=True),
        lax.all_to_all(
            send_count[0].astype(jnp.bfloat16), "col", split_axis=0, concat_axis=0, tiled=True
        ),
    )
    live_slots = (
        jnp.arange(slot_count, dtype=jnp.int32)[None, :] < arrived_count.astype(jnp.int32)[:, None]
    ).reshape(-1)
    halo_used = jnp.where(live_slots[None, :], halo_weight, jnp.zeros((), jnp.bfloat16))
    local_sum = jnp.dot(local_weight, features, preferred_element_type=jnp.float32)
    halo_sum = jnp.dot(
        halo_used, arrived.reshape(-1, feat_width), preferred_element_type=jnp.float32
    )
    hub_sum = jnp.dot(
        hub_weight,
        lax.all_gather(hub_local, ("row", "col"), axis=0, tiled=True),
        preferred_element_type=jnp.float32,
    )
    degree = (
        1.0
        + jnp.sum(local_weight.astype(jnp.float32), axis=1)
        + jnp.sum(hub_weight.astype(jnp.float32), axis=1)
        + jnp.sum(halo_used.astype(jnp.float32), axis=1)
    )
    neigh = ((local_sum + hub_sum + halo_sum) / degree[:, None]).astype(jnp.bfloat16)
    preact = jnp.dot(features, w_self, preferred_element_type=jnp.float32) + jnp.dot(
        neigh, w_neigh, preferred_element_type=jnp.float32
    )
    sigmoid_pre = jax.nn.sigmoid(preact)
    output = (preact * sigmoid_pre).astype(jnp.bfloat16)
    grad_pre = (
        grad_out.astype(jnp.float32) * (sigmoid_pre + preact * sigmoid_pre * (1.0 - sigmoid_pre))
    ).astype(jnp.bfloat16)
    part_self = jnp.dot(features.T, grad_pre, preferred_element_type=jnp.float32)
    part_neigh = jnp.dot(neigh.T, grad_pre, preferred_element_type=jnp.float32)
    grad_agg = (
        jnp.dot(grad_pre, w_neigh.T, preferred_element_type=jnp.float32) / degree[:, None]
    ).astype(jnp.bfloat16)
    grad_local = jnp.dot(grad_pre, w_self.T, preferred_element_type=jnp.float32) + jnp.dot(
        local_weight.T, grad_agg, preferred_element_type=jnp.float32
    )
    halo_back = jnp.dot(halo_used.T, grad_agg, preferred_element_type=jnp.float32).reshape(
        peer_count, slot_count, feat_width
    )
    returned = lax.all_to_all(
        halo_back.astype(jnp.bfloat16), "col", split_axis=0, concat_axis=0, tiled=True
    ).astype(halo_back.dtype)
    grad_total = grad_local.at[send_index].add(returned.reshape(-1, feat_width))
    hub_count = hub_local.shape[0]
    hub_partial = jnp.dot(hub_weight.T, grad_agg, preferred_element_type=jnp.float32)
    hub_total, grad_self, grad_neigh = lax.psum(
        (hub_partial, part_self, part_neigh), ("row", "col")
    )
    own_hub_grad = lax.dynamic_slice_in_dim(
        hub_total, lax.axis_index(("row", "col")) * hub_count, hub_count, 0
    )
    grad_total = grad_total.at[hub_rows[0]].add(own_hub_grad)
    return (output, grad_total.astype(jnp.bfloat16), grad_self, grad_neigh)


def solution(mesh):
    in_specs = (
        P(("row", "col"), None),
        P(),
        P(),
        P(("row", "col"), None),
        P(("row", "col"), None),
        P(("row", "col"), None),
        P(("row", "col"), None, None),
        P(("row", "col"), None),
        P(("row", "col"), None),
        P(("row", "col"), None),
    )
    out_specs = (P(("row", "col"), None), P(("row", "col"), None), P(), P())
    return jax.shard_map(
        per_device, mesh=mesh, in_specs=in_specs, out_specs=out_specs, check_vma=False
    )
```

profile of v0, /device:TPU:1, one launch (start us, length us, event | category | flops | bytes accessed | tf_op | source)
XLA Modules:
  0.0 432.2 jit_solution(10765986551507175164)
XLA Ops:
  7.2 0.7 convert_bitcast_fusion
  8.6 17.4 %all-to-all-start = ((bf16[16,1,1]{2,1,0:T(2,128)(2,1)}), bf16[16,1,1]{2,1,0:T(2,128)(2,1)S(1)}, u32[]{:S(2)}, u32[]{:S(2)}) async-start(bf16[16,1,1]{2,1,0:T(2,128)(2,1)} %copy.28), calls=%async_computation | async-start | bytes 16384 | tf_op jit(solution)/shard_map/all_to_all | solution.py:27
  26.0 1.2 convert_reduce_fusion.1
  27.2 2.1 fusion.17
  29.4 1.0 fusion.16
  31.2 82.1 %all-gather = bf16[1024,1,256]{2,1,0:T(2,128)(2,1)S(1)} all-gather(bf16[1,1,256]{2,1,0:T(2,128)(2,1)S(1)} %dynamic-slice_bitcast_fusion), channel_id=1, replica_groups=mesh['row'=64,'col'=16] {'row','col'}, dimensions={0}, use_global_device_ids=true | all-gather | bytes 524800 | tf_op jit(solution)/shard_map/all_gather | solution.py:41
  113.5 1.8 gather_fusion
  115.3 5.9 %all-to-all-start.1 = ((bf16[16,16,256]{2,1,0:T(8,128)(2,1)}), bf16[16,16,256]{2,1,0:T(8,128)(2,1)S(1)}, u32[]{:S(2)}, u32[]{:S(2)}) async-start(bf16[16,16,256]{2,1,0:T(8,128)(2,1)} %bitcast.6), calls=%async_computation.1 | async-start | bytes 262144 | tf_op jit(solution)/shard_map/all_to_all | solution.py:26
  122.0 8.4 %all-to-all-done.1 = bf16[16,16,256]{2,1,0:T(8,128)(2,1)S(1)} async-done(((bf16[16,16,256]{2,1,0:T(8,128)(2,1)}), bf16[16,16,256]{2,1,0:T(8,128)(2,1)S(1)}, u32[]{:S(2)}, u32[]{:S(2)}) %all-to-all-start.1) | async-done | bytes 131104 | tf_op jit(solution)/shard_map/all_to_all | solution.py:26
  130.6 1.6 fusion.3
  132.2 1.1 multiply_convert_fusion
  133.6 1.0 convolution_bitcast_fusion.3
  134.6 1.0 fusion.18
  135.6 1.6 convolution_bitcast_fusion
  137.8 0.8 and_reduce_fusion
  138.6 0.9 convolution_convert_fusion
  139.5 3.4 all-to-all-start.2
  143.6 8.2 %all-to-all-done.2 = bf16[16,16,256]{2,1,0:T(8,128)(2,1)S(1)} async-done(((bf16[16,16,256]{2,1,0:T(8,128)(2,1)}), bf16[16,16,256]{2,1,0:T(8,128)(2,1)S(1)}, u32[]{:S(2)}, u32[]{:S(2)}) %all-to-all-start.2) | async-done | bytes 131104 | tf_op jit(solution)/shard_map/all_to_all | solution.py:70
  151.8 2.2 scatter_custom_fusion
  154.0 266.6 %all-reduce.3.cloned.1.call-done = (f32[1024,256]{1,0:T(8,128)}, f32[256,256]{0,1:T(8,128)}, f32[256,256]{1,0:T(8,128)}) async-done(((f32[1024,256]{1,0:T(8,128)}, f32[256,256]{0,1:T(8,128)}, f32[256,256]{1,0:T(8,128)}), (f32[1024,256]{1,0:T(8,128)}, f32[256,256]{0,1:T(8,128)}, f32[256,256]{1,0:T(8,128)})) %all-reduce.3.cloned.1.call-update) | async-done | bytes 1572880 | tf_op jit(solution)/shard_map/psum | solution.py:76
  420.6 1.4 broadcast_select_fusion.3
  422.1 0.7 convert_element_type.71
  422.8 1.8 copy.31
  424.6 0.7 copy.46
  (41 shorter events, 3.6 us)
Async XLA Ops:
  7.2 20.0 %copy-start = (bf16[512,256]{1,0:T(8,128)(2,1)S(1)}, bf16[512,256]{1,0:T(8,128)(2,1)}, u32[]{:S(2)}) copy-start(bf16[512,256]{1,0:T(8,128)(2,1)} %param.12) | copy-start | bytes 786436
  7.2 22.2 %copy-start.5 = (bf16[256,256]{1,0:T(8,128)(2,1)S(1)}, bf16[256,256]{1,0:T(8,128)(2,1)}, u32[]{:S(2)}) copy-start(bf16[256,256]{1,0:T(8,128)(2,1)} %param.13) | copy-start | bytes 393220
  8.6 106.7 %all-to-all-start = ((bf16[16,1,1]{2,1,0:T(2,128)(2,1)}), bf16[16,1,1]{2,1,0:T(2,128)(2,1)S(1)}, u32[]{:S(2)}, u32[]{:S(2)}) async-start(bf16[16,1,1]{2,1,0:T(2,128)(2,1)} %copy.28), calls=%async_computation | async-start | bytes 16384 | tf_op jit(solution)/shard_map/all_to_all | solution.py:27
  27.2 3.2 copy-start.7
  29.4 83.9 %copy-start.2 = (bf16[512,1024]{1,0:T(8,128)(2,1)S(1)}, bf16[512,1024]{1,0:T(8,128)(2,1)}, u32[]{:S(2)}) copy-start(bf16[512,1024]{1,0:T(8,128)(2,1)} %param.17) | copy-start | bytes 3145732
  113.3 8.5 %copy-start.3 = (bf16[512,256]{1,0:T(8,128)(2,1)S(1)}, bf16[512,256]{1,0:T(8,128)(2,1)}, u32[]{:S(2)}) copy-start(bf16[512,256]{1,0:T(8,128)(2,1)} %param.20) | copy-start | bytes 786436
  115.3 15.1 %all-to-all-start.1 = ((bf16[16,16,256]{2,1,0:T(8,128)(2,1)}), bf16[16,16,256]{2,1,0:T(8,128)(2,1)S(1)}, u32[]{:S(2)}, u32[]{:S(2)}) async-start(bf16[16,16,256]{2,1,0:T(8,128)(2,1)} %bitcast.6), calls=%async_computation.1 | async-start | bytes 262144 | tf_op jit(solution)/shard_map/all_to_all | solution.py:26
  121.2 299.4 %all-reduce.3.cloned.1.call-start = ((), (), s32[]{:S(2)}) async-start(), calls=%async_computation.3 | async-start | bytes 3145728 | tf_op jit(solution)/shard_map/psum | solution.py:76
  130.6 1.6 copy-start.4
  130.6 1.6 copy-start.9
  130.6 1.6 copy-start.10
  137.1 0.7 copy-start.8
  137.1 5.8 %copy-start.1 = (bf16[512,512]{1,0:T(8,128)(2,1)S(1)}, bf16[512,512]{1,0:T(8,128)(2,1)}, u32[]{:S(2)}) copy-start(bf16[512,512]{1,0:T(8,128)(2,1)} %param.15) | copy-start | bytes 1572868
  139.5 12.3 %all-to-all-start.2 = ((bf16[16,16,256]{2,1,0:T(8,128)(2,1)}), bf16[16,16,256]{2,1,0:T(8,128)(2,1)S(1)}, u32[]{:S(2)}, u32[]{:S(2)}) async-start(bf16[16,16,256]{2,1,0:T(8,128)(2,1)} %bitcast.9), calls=%async_computation.2 | async-start | bytes 262144 | tf_op jit(solution)/shard_map/all_to_all | solution.py:70
  420.6 4.0 copy-start.6
Sparse Core Ops, SparseCore 0:
  137.3 283.2 all-reduce.2
where the time goes:
time: 433 us; the launch traced here: 432 us
  waiting for transfers between devices  283 us (65%)
  blocking collectives  82.1 us (19%)
  starting transfers between devices  26.8 us (6%)
  between operations  14.9 us (3%)
  matrix products  11.4 us (3%)
  other arithmetic  7.87 us (2%)
  local copies, waits for them, and re-layouts  5.88 us (1%)
    psum x1, waiting for transfers between devices, per_device(): lax.psum((hub_partial, part_self, part_neigh), ('row', 'col'))  267 us
    all_gather x1, blocking collectives, per_device(): lax.all_gather(hub_local, ('row', 'col'), axis=0, tiled=True)  82.1 us
    all_to_all x1, starting transfers between devices, per_device(): lax.all_to_all(send_count[0].astype(jnp.bfloat16), 'col', split_axis=0, c...  17.4 us
  transfers between devices with their start and end apart: 4, of which 3 were waited for; matrix products, arithmetic and copies ran while one was open for 3% of the time, Pallas kernels for 0%

commit v1 on v0

v1 whole, which is shorter than its diff:
```python
import jax
import jax.numpy as jnp
from jax import lax
from jax.sharding import PartitionSpec as P

F32 = jnp.float32
BF16 = jnp.bfloat16


def dot(a, b):
    return jnp.dot(a, b, preferred_element_type=F32)


def dot_t(a, b):
    return lax.dot_general(a, b, (((0,), (0,)), ((), ())), preferred_element_type=F32)


def dot_nt(a, b):
    return lax.dot_general(a, b, (((1,), (1,)), ((), ())), preferred_element_type=F32)


def exchange(x, axis):
    return lax.all_to_all(x, axis, split_axis=0, concat_axis=0, tiled=True)


def per_device(
    features,
    w_self,
    w_neigh,
    local_weight,
    hub_rows,
    hub_weight,
    send_rows,
    send_count,
    halo_weight,
    grad_out,
):
    nodes, feat = features.shape
    peers, slots = send_rows.shape[1:]
    groups = lax.axis_size("row")
    hubs = hub_weight.shape[1]
    row_ids = jnp.arange(nodes, dtype=jnp.int32)

    pick = jnp.concatenate(
        [
            send_rows[0],
            jnp.broadcast_to(hub_rows, (peers, 1)),
            jnp.full((peers, 1), -1, jnp.int32),
        ],
        axis=1,
    )
    pick_hot = (pick[:, :, None] == row_ids).astype(BF16).reshape(-1, nodes)
    message = dot(pick_hot, features).astype(BF16).reshape(peers, slots + 2, feat)
    count_slot = (jnp.arange(slots + 2) == slots + 1)[None, :, None]
    message = jnp.where(count_slot, send_count[0].astype(BF16)[:, None, None], message)
    got = exchange(message, "col")
    halo_feat = got[:, :slots].reshape(peers * slots, feat)
    group_hubs = got[:, slots]
    counts = got[:, slots + 1, 0].astype(jnp.int32)
    hub_feat = exchange(
        jnp.broadcast_to(group_hubs[None], (groups, peers, feat)), "row"
    ).reshape(hubs, feat)

    live = (jnp.arange(slots, dtype=jnp.int32)[None, :] < counts[:, None]).reshape(-1)
    halo_used = jnp.where(live[None, :], halo_weight, jnp.zeros((), BF16))
    degree = (
        1.0
        + jnp.sum(local_weight.astype(F32), axis=1)
        + jnp.sum(hub_weight.astype(F32), axis=1)
        + jnp.sum(halo_used.astype(F32), axis=1)
    )[:, None]
    agg_sum = dot(local_weight, features) + dot(halo_used, halo_feat) + dot(hub_weight, hub_feat)
    neigh = (agg_sum / degree).astype(BF16)
    preact = dot(features, w_self) + dot(neigh, w_neigh)
    sig = jax.nn.sigmoid(preact)
    output = (preact * sig).astype(BF16)
    grad_pre = (grad_out.astype(F32) * (sig + preact * sig * (1.0 - sig))).astype(BF16)
    part_self = dot_t(features, grad_pre).astype(BF16)
    part_neigh = dot_t(neigh, grad_pre).astype(BF16)
    grad_agg = (dot_nt(grad_pre, w_neigh) / degree).astype(BF16)
    hub_partial = dot_t(hub_weight, grad_agg).astype(BF16)
    weights = jnp.concatenate([part_self, part_neigh], axis=0).reshape(groups, -1, feat)
    share = weights.shape[1]
    partial = jnp.concatenate([hub_partial.reshape(groups, peers, feat), weights], axis=1)
    row_sum = jnp.sum(exchange(partial, "row").astype(F32), axis=0).astype(BF16)

    grad_local = dot_nt(grad_pre, w_self) + dot_t(local_weight, grad_agg)
    halo_back = dot_t(halo_used, grad_agg).astype(BF16).reshape(peers, slots, feat)
    back = exchange(
        jnp.concatenate(
            [
                halo_back,
                row_sum[:peers, None],
                jnp.broadcast_to(row_sum[None, peers:], (peers, share, feat)),
            ],
            axis=1,
        ),
        "col",
    )
    weight_sum = jnp.sum(back[:, slots + 1 :].astype(F32), axis=0).astype(BF16)
    all_weights = exchange(
        jnp.broadcast_to(weight_sum[None], (groups, share, feat)), "row"
    ).reshape(-1, feat).astype(F32)

    returned = back[:, :slots].reshape(-1, feat)
    send_hot = (send_rows[0].reshape(-1)[:, None] == row_ids).astype(BF16)
    own_hub = jnp.sum(back[:, slots].astype(F32), axis=0)
    grad_total = grad_local + dot_t(send_hot, returned)
    grad_total = grad_total + jnp.where((row_ids == hub_rows[0, 0])[:, None], own_hub, 0.0)
    return (
        output,
        grad_total.astype(BF16),
        all_weights[:feat],
        all_weights[feat:],
    )


def solution(mesh):
    rows = P(("row", "col"), None)
    in_specs = (
        rows,
        P(),
        P(),
        rows,
        rows,
        rows,
        P(("row", "col"), None, None),
        rows,
        rows,
        rows,
    )
    return jax.shard_map(
        per_device, mesh=mesh, in_specs=in_specs, out_specs=(rows, rows, P(), P()), check_vma=False
    )
```

time: 433 us -> 140 us (0.32)
  waiting for transfers between devices: 283 us -> 70.5 us
  blocking collectives: 82.1 us -> 0 us
  starting transfers between devices: 26.8 us -> 51.6 us
  between operations: 14.9 us -> 1.61 us
    psum x1 -> x0, waiting for transfers between devices: 267 us -> none  [per_device(): lax.psum((hub_partial, part_self, part_neigh), ('row', 'col'))]
    all_gather x1 -> x0, blocking collectives: 82.1 us -> none  [per_device(): lax.all_gather(hub_local, ('row', 'col'), axis=0, tiled=True)]
    all_to_all x3 -> x5, waiting for transfers between devices: 16.6 us -> 70.5 us  [exchange(): return lax.all_to_all(x, axis, split_axis=0, concat_axis=0, tiled=True)]
    all_to_all x3 -> x5, starting transfers between devices: 26.7 us -> 51.6 us  [exchange(): return lax.all_to_all(x, axis, split_axis=0, concat_axis=0, tiled=True)]
    dot_general x12 -> x14, matrix products: 11.4 us -> 7.74 us  [the longest x6 4.49 us: dot(): return jnp.dot(a, b, preferred_element_type=F32)]
  transfers between devices with their start and end apart: 4 -> 5, of which waited for: 3 -> 5; matrix products, arithmetic and copies ran while one was open for 3% -> 3% of each run, Pallas kernels for 0% -> 0%
where the time goes in v1:
time: 140 us
  waiting for transfers between devices  70.5 us (50%)
  starting transfers between devices  51.6 us (37%)
  matrix products  7.74 us (6%)
  other arithmetic  5.13 us (4%)
  local copies, waits for them, and re-layouts  3.18 us (2%)
  between operations  1.61 us (1%)
    all_to_all x5, waiting for transfers between devices, exchange(): return lax.all_to_all(x, axis, split_axis=0, concat_axis=0, tiled=True)  70.5 us
    all_to_all x5, starting transfers between devices, exchange(): return lax.all_to_all(x, axis, split_axis=0, concat_axis=0, tiled=True)  51.6 us
    dot_general x6, matrix products, dot(): return jnp.dot(a, b, preferred_element_type=F32)  4.49 us
  transfers between devices with their start and end apart: 5, of which 5 were waited for; matrix products, arithmetic and copies ran while one was open for 3% of the time, Pallas kernels for 0%

profile of v1, /device:TPU:1, one launch (start us, length us, event | category | flops | bytes accessed | tf_op | source)
XLA Modules:
  0.0 139.7 jit_solution(14532676461367342263)
XLA Ops:
  1.5 0.7 add_add_fusion
  2.7 0.7 convert_bitcast_fusion
  3.4 0.8 broadcast_select_fusion.3
  4.2 17.5 %all-to-all-start = ((bf16[16,18,256]{2,1,0:T(8,128)(2,1)}), bf16[16,18,256]{2,1,0:T(8,128)(2,1)S(1)}, u32[]{:S(2)}, u32[]{:S(2)}) async-start(bf16[16,18,256]{2,1,0:T(8,128)(2,1)} %broadcast_select_fusion.3), calls=%async_computation | async-start | bytes 393216 | tf_op jit(solution)/shard_map/all_to_all | solution.py:23
  21.7 1.0 fusion.18
  23.2 8.8 %all-to-all-done = bf16[16,18,256]{2,1,0:T(8,128)(2,1)S(1)} async-done(((bf16[16,18,256]{2,1,0:T(8,128)(2,1)}), bf16[16,18,256]{2,1,0:T(8,128)(2,1)S(1)}, u32[]{:S(2)}, u32[]{:S(2)}) %all-to-all-start) | async-done | bytes 147488 | tf_op jit(solution)/shard_map/all_to_all | solution.py:23
  32.1 0.8 broadcast_in_dim.89
  32.9 14.3 %all-to-all-start.1 = ((bf16[64,16,256]{2,1,0:T(8,128)(2,1)}), bf16[64,16,256]{2,1,0:T(8,128)(2,1)}, u32[]{:S(2)}, u32[]{:S(2)}) async-start(bf16[64,16,256]{2,1,0:T(8,128)(2,1)} %broadcast_in_dim.89), calls=%async_computation.1 | async-start | bytes 1048576 | tf_op jit(solution)/shard_map/all_to_all | solution.py:23
  47.3 0.4 fusion.15
  48.3 16.6 %all-to-all-done.1 = bf16[64,16,256]{2,1,0:T(8,128)(2,1)} async-done(((bf16[64,16,256]{2,1,0:T(8,128)(2,1)}), bf16[64,16,256]{2,1,0:T(8,128)(2,1)}, u32[]{:S(2)}, u32[]{:S(2)}) %all-to-all-start.1) | async-done | bytes 524320 | tf_op jit(solution)/shard_map/all_to_all | solution.py:23
  64.9 1.6 %fusion.5 = bf16[512,256]{1,0:T(8,128)(2,1)S(1)} fusion(f32[512,256]{1,0:T(8,128)S(1)} %convolution_add_fusion.3, bf16[512,1024]{1,0:T(8,128)(2,1)S(1)} %copy-done.2, bf16[1024,256]{1,0:T(8,128)(2,1)} %bitcast.4, f32[512]{0:T(512)S(1)} %add_add_fusion.1), kind=kOutput, calls=%fused_computation.14 | convolution fusion | flops 268828672 | bytes 2361344 | tf_op jit(solution)/shard_map/dot_general | solution.py:11
  66.5 1.1 multiply_convert_fusion
  68.5 0.5 fusion
  69.2 0.9 pad_maximum_fusion
  70.1 6.5 %all-to-all-start.2 = ((bf16[64,24,256]{2,1,0:T(8,128)(2,1)}), bf16[64,24,256]{2,1,0:T(8,128)(2,1)S(1)}, u32[]{:S(2)}, u32[]{:S(2)}) async-start(bf16[64,24,256]{2,1,0:T(8,128)(2,1)} %pad_maximum_fusion), calls=%async_computation.2 | async-start | bytes 1572864 | tf_op jit(solution)/shard_map/all_to_all | solution.py:23
  76.9 20.9 %all-to-all-done.2 = bf16[64,24,256]{2,1,0:T(8,128)(2,1)S(1)} async-done(((bf16[64,24,256]{2,1,0:T(8,128)(2,1)}), bf16[64,24,256]{2,1,0:T(8,128)(2,1)S(1)}, u32[]{:S(2)}, u32[]{:S(2)}) %all-to-all-start.2) | async-done | bytes 786464 | tf_op jit(solution)/shard_map/all_to_all | solution.py:23
  98.0 0.8 pad_maximum_fusion.1
  98.8 7.6 %all-to-all-start.3 = ((bf16[16,25,256]{2,1,0:T(8,128)(2,1)}), bf16[16,25,256]{2,1,0:T(8,128)(2,1)S(1)}, u32[]{:S(2)}, u32[]{:S(2)}) async-start(bf16[16,25,256]{2,1,0:T(8,128)(2,1)} %pad_maximum_fusion.1), calls=%async_computation.3 | async-start | bytes 524288 | tf_op jit(solution)/shard_map/all_to_all | solution.py:23
  106.8 11.4 %all-to-all-done.3 = bf16[16,25,256]{2,1,0:T(8,128)(2,1)S(1)} async-done(((bf16[16,25,256]{2,1,0:T(8,128)(2,1)}), bf16[16,25,256]{2,1,0:T(8,128)(2,1)S(1)}, u32[]{:S(2)}, u32[]{:S(2)}) %all-to-all-start.3) | async-done | bytes 204832 | tf_op jit(solution)/shard_map/all_to_all | solution.py:23
  118.2 0.7 broadcast_in_dim.95
  118.9 5.7 %all-to-all-start.4 = ((bf16[64,8,256]{2,1,0:T(8,128)(2,1)}), bf16[64,8,256]{2,1,0:T(8,128)(2,1)S(1)}, u32[]{:S(2)}, u32[]{:S(2)}) async-start(bf16[64,8,256]{2,1,0:T(8,128)(2,1)} %broadcast_in_dim.95), calls=%async_computation.4 | async-start | bytes 524288 | tf_op jit(solution)/shard_map/all_to_all | solution.py:23
  125.0 1.1 fusion.4
  126.1 12.7 %all-to-all-done.4 = bf16[64,8,256]{2,1,0:T(8,128)(2,1)S(1)} async-done(((bf16[64,8,256]{2,1,0:T(8,128)(2,1)}), bf16[64,8,256]{2,1,0:T(8,128)(2,1)S(1)}, u32[]{:S(2)}, u32[]{:S(2)}) %all-to-all-start.4) | async-done | bytes 262176 | tf_op jit(solution)/shard_map/all_to_all | solution.py:23
  138.9 0.8 slice_bitcast_fusion
  (54 shorter events, 4.1 us)
Async XLA Ops:
  0.6 1.7 %copy-start = (bf16[512,256]{1,0:T(8,128)(2,1)S(1)}, bf16[512,256]{1,0:T(8,128)(2,1)}, u32[]{:S(2)}) copy-start(bf16[512,256]{1,0:T(8,128)(2,1)} %param.10) | copy-start | bytes 786436
  0.6 21.0 %copy-start.5 = (bf16[256,256]{1,0:T(8,128)(2,1)S(1)}, bf16[256,256]{1,0:T(8,128)(2,1)}, u32[]{:S(2)}) copy-start(bf16[256,256]{1,0:T(8,128)(2,1)} %param.11) | copy-start | bytes 393220
  2.6 20.1 %copy-start.2 = (bf16[512,1024]{1,0:T(8,128)(2,1)S(1)}, bf16[512,1024]{1,0:T(8,128)(2,1)}, u32[]{:S(2)}) copy-start(bf16[512,1024]{1,0:T(8,128)(2,1)} %param.15) | copy-start | bytes 3145732
  4.2 27.8 %all-to-all-start = ((bf16[16,18,256]{2,1,0:T(8,128)(2,1)}), bf16[16,18,256]{2,1,0:T(8,128)(2,1)S(1)}, u32[]{:S(2)}, u32[]{:S(2)}) async-start(bf16[16,18,256]{2,1,0:T(8,128)(2,1)} %broadcast_select_fusion.3), calls=%async_computation | async-start | bytes 393216 | tf_op jit(solution)/shard_map/all_to_all | solution.py:23
  21.7 1.2 copy-start.1
  32.9 15.0 %copy-start.3 = (bf16[512,256]{1,0:T(8,128)(2,1)S(1)}, bf16[512,256]{1,0:T(8,128)(2,1)}, u32[]{:S(2)}) copy-start(bf16[512,256]{1,0:T(8,128)(2,1)} %param.18) | copy-start | bytes 786436
  32.9 32.0 %all-to-all-start.1 = ((bf16[64,16,256]{2,1,0:T(8,128)(2,1)}), bf16[64,16,256]{2,1,0:T(8,128)(2,1)}, u32[]{:S(2)}, u32[]{:S(2)}) async-start(bf16[64,16,256]{2,1,0:T(8,128)(2,1)} %broadcast_in_dim.89), calls=%async_computation.1 | async-start | bytes 1048576 | tf_op jit(solution)/shard_map/all_to_all | solution.py:23
  64.9 1.6 %copy-start.4 = (f32[512,256]{1,0:T(8,128)S(1)}, f32[512,256]{1,0:T(8,128)}, u32[]{:S(2)}) copy-start(f32[512,256]{1,0:T(8,128)} %fusion.18) | copy-start | bytes 1572868
  64.9 1.6 %copy-start.7 = (bf16[512,256]{1,0:T(8,128)(2,1)S(1)}, bf16[512,256]{1,0:T(8,128)(2,1)}, u32[]{:S(2)}) copy-start(bf16[512,256]{1,0:T(8,128)(2,1)} %param.19) | copy-start | bytes 786436
  64.9 1.6 %copy-start.8 = (bf16[256,256]{1,0:T(8,128)(2,1)S(1)}, bf16[256,256]{1,0:T(8,128)(2,1)}, u32[]{:S(2)}) copy-start(bf16[256,256]{1,0:T(8,128)(2,1)} %param.12) | copy-start | bytes 393220
  70.1 27.7 %all-to-all-start.2 = ((bf16[64,24,256]{2,1,0:T(8,128)(2,1)}), bf16[64,24,256]{2,1,0:T(8,128)(2,1)S(1)}, u32[]{:S(2)}, u32[]{:S(2)}) async-start(bf16[64,24,256]{2,1,0:T(8,128)(2,1)} %pad_maximum_fusion), calls=%async_computation.2 | async-start | bytes 1572864 | tf_op jit(solution)/shard_map/all_to_all | solution.py:23
  76.9 29.4 %copy-start.6 = (s32[1,16,16]{2,1,0:T(8,128)S(1)}, s32[1,16,16]{2,1,0:T(8,128)}, u32[]{:S(2)}) copy-start(s32[1,16,16]{2,1,0:T(8,128)} %param.16) | copy-start | bytes 3076
  98.8 19.4 %all-to-all-start.3 = ((bf16[16,25,256]{2,1,0:T(8,128)(2,1)}), bf16[16,25,256]{2,1,0:T(8,128)(2,1)S(1)}, u32[]{:S(2)}, u32[]{:S(2)}) async-start(bf16[16,25,256]{2,1,0:T(8,128)(2,1)} %pad_maximum_fusion.1), calls=%async_computation.3 | async-start | bytes 524288 | tf_op jit(solution)/shard_map/all_to_all | solution.py:23
  118.9 19.9 %all-to-all-start.4 = ((bf16[64,8,256]{2,1,0:T(8,128)(2,1)}), bf16[64,8,256]{2,1,0:T(8,128)(2,1)S(1)}, u32[]{:S(2)}, u32[]{:S(2)}) async-start(bf16[64,8,256]{2,1,0:T(8,128)(2,1)} %broadcast_in_dim.95), calls=%async_computation.4 | async-start | bytes 524288 | tf_op jit(solution)/shard_map/all_to_all | solution.py:23

commit v2 on v1

--- a/solution.py
+++ b/solution.py
@@ -57,8 +57,14 @@
     halo_feat = got[:, :slots].reshape(peers * slots, feat)
     group_hubs = got[:, slots]
     counts = got[:, slots + 1, 0].astype(jnp.int32)
-    hub_feat = exchange(
-        jnp.broadcast_to(group_hubs[None], (groups, peers, feat)), "row"
+    half, cols = peers // 2, feat // 2
+    core = lax.axis_index("col") % 2
+    swap = [(i, i ^ 1) for i in range(peers)]
+    half_hubs = jnp.where(core == 0, group_hubs[:half], group_hubs[half:])
+    held = exchange(jnp.broadcast_to(half_hubs[None], (groups, half, feat)), "row")
+    other = lax.ppermute(held, "col", swap)
+    hub_feat = jnp.concatenate(
+        [jnp.where(core == 0, held, other), jnp.where(core == 0, other, held)], axis=1
     ).reshape(hubs, feat)
 
     live = (jnp.arange(slots, dtype=jnp.int32)[None, :] < counts[:, None]).reshape(-1)
@@ -75,29 +81,48 @@
     sig = jax.nn.sigmoid(preact)
     output = (preact * sig).astype(BF16)
     grad_pre = (grad_out.astype(F32) * (sig + preact * sig * (1.0 - sig))).astype(BF16)
-    part_self = dot_t(features, grad_pre).astype(BF16)
-    part_neigh = dot_t(neigh, grad_pre).astype(BF16)
+    part_self = dot_t(features, grad_pre)
+    part_neigh = dot_t(neigh, grad_pre)
     grad_agg = (dot_nt(grad_pre, w_neigh) / degree).astype(BF16)
-    hub_partial = dot_t(hub_weight, grad_agg).astype(BF16)
+    hub_partial = dot_t(hub_weight, grad_agg)
+
+    hub_halves = hub_partial.reshape(groups, 2, half, feat)
     weights = jnp.concatenate([part_self, part_neigh], axis=0).reshape(groups, -1, feat)
     share = weights.shape[1]
-    partial = jnp.concatenate([hub_partial.reshape(groups, peers, feat), weights], axis=1)
-    row_sum = jnp.sum(exchange(partial, "row").astype(F32), axis=0).astype(BF16)
+
+    def piece(which):
+        hub = jnp.where(which == 0, hub_halves[:, 0], hub_halves[:, 1])
+        weight = jnp.where(which == 0, weights[:, :, :cols], weights[:, :, cols:])
+        return jnp.concatenate([hub, weight], axis=2).astype(BF16)
+
+    theirs = lax.ppermute(piece(1 - core), "col", swap)
+    paired = (piece(core).astype(F32) + theirs.astype(F32)).astype(BF16)
+    row_sum = jnp.sum(exchange(paired, "row").astype(F32), axis=0).astype(BF16)
 
     grad_local = dot_nt(grad_pre, w_self) + dot_t(local_weight, grad_agg)
     halo_back = dot_t(halo_used, grad_agg).astype(BF16).reshape(peers, slots, feat)
+    mine = (jnp.arange(peers) // half == core)[:, None, None]
+    own_hubs = jnp.concatenate([row_sum[:, :feat]] * 2, axis=0)[:, None]
+    own_hubs = jnp.where(mine, own_hubs, jnp.zeros((), BF16))
+    fold = share // 2
+    own_weights = jnp.concatenate([row_sum[:fold, feat:], row_sum[fold:, feat:]], axis=1)
     back = exchange(
         jnp.concatenate(
-            [
-                halo_back,
-                row_sum[:peers, None],
-                jnp.broadcast_to(row_sum[None, peers:], (peers, share, feat)),
-            ],
+            [halo_back, own_hubs, jnp.broadcast_to(own_weights[None], (peers, fold, feat))],
             axis=1,
         ),
         "col",
     )
-    weight_sum = jnp.sum(back[:, slots + 1 :].astype(F32), axis=0).astype(BF16)
+    weight_sum = jnp.sum(
+        back[:, slots + 1 :].astype(F32).reshape(half, 2, fold, feat), axis=0
+    ).astype(BF16)
+    weight_sum = jnp.concatenate(
+        [
+            jnp.concatenate([weight_sum[0, :, :cols], weight_sum[1, :, :cols]], axis=1),
+            jnp.concatenate([weight_sum[0, :, cols:], weight_sum[1, :, cols:]], axis=1),
+        ],
+        axis=0,
+    )
     all_weights = exchange(
         jnp.broadcast_to(weight_sum[None], (groups, share, feat)), "row"
     ).reshape(-1, feat).astype(F32)

time: 140 us -> 132 us (0.943)
  waiting for transfers between devices: 70.5 us -> 61.7 us
    all_to_all x5, waiting for transfers between devices: 70.5 us -> 59.5 us  [exchange(): return lax.all_to_all(x, axis, split_axis=0, concat_axis=0, tiled=True)]
    ppermute x0 -> x2, starting transfers between devices: none -> 5.89 us  [the longest x1 3.61 us: per_device(): other = lax.ppermute(held, 'col', swap)]
    all_to_all x5, starting transfers between devices: 51.6 us -> 46.4 us  [exchange(): return lax.all_to_all(x, axis, split_axis=0, concat_axis=0, tiled=True)]
    ppermute x0 -> x2, waiting for transfers between devices: none -> 2.2 us  [the longest x1 1.33 us: per_device(): theirs = lax.ppermute(piece(1 - core), 'col', swap)]
  transfers between devices with their start and end apart: 5 -> 7, of which waited for: 5 -> 7; matrix products, arithmetic and copies ran while one was open for 3% -> 4% of each run, Pallas kernels for 0% -> 0%
where the time goes in v2:
time: 132 us; the launch traced here: 131 us
  waiting for transfers between devices  61.7 us (47%)
  starting transfers between devices  52.3 us (40%)
  matrix products  6.63 us (5%)
  other arithmetic  5.28 us (4%)
  local copies, waits for them, and re-layouts  3.73 us (3%)
  between operations  1.72 us (1%)
    all_to_all x5, waiting for transfers between devices, exchange(): return lax.all_to_all(x, axis, split_axis=0, concat_axis=0, tiled=True)  59.5 us
    all_to_all x5, starting transfers between devices, exchange(): return lax.all_to_all(x, axis, split_axis=0, concat_axis=0, tiled=True)  46.4 us
    ppermute x1, starting transfers between devices, per_device(): other = lax.ppermute(held, 'col', swap)  3.61 us
    dot_general x6, matrix products, dot(): return jnp.dot(a, b, preferred_element_type=F32)  3.38 us
    dot_general x6, matrix products, dot_t(): lax.dot_general(a, b, (((0,), (0,)), ((), ())), preferred_element_type=F32)  2.72 us
  transfers between devices with their start and end apart: 7, of which 7 were waited for; matrix products, arithmetic and copies ran while one was open for 4% of the time, Pallas kernels for 0%

profile of v2, /device:TPU:1, one launch (start us, length us, event | category | flops | bytes accessed | tf_op | source)
XLA Modules:
  0.0 131.4 jit_solution(11991821420457460623)
XLA Ops:
  2.7 0.7 convert_bitcast_fusion
  3.4 0.8 broadcast_select_fusion.5
  4.2 17.5 %all-to-all-start = ((bf16[16,18,256]{2,1,0:T(8,128)(2,1)}), bf16[16,18,256]{2,1,0:T(8,128)(2,1)S(1)}, u32[]{:S(2)}, u32[]{:S(2)}) async-start(bf16[16,18,256]{2,1,0:T(8,128)(2,1)} %broadcast_select_fusion.5), calls=%async_computation | async-start | bytes 393216 | tf_op jit(solution)/shard_map/all_to_all | solution.py:23
  21.7 1.0 fusion.20
  23.2 8.8 %all-to-all-done = bf16[16,18,256]{2,1,0:T(8,128)(2,1)S(1)} async-done(((bf16[16,18,256]{2,1,0:T(8,128)(2,1)}), bf16[16,18,256]{2,1,0:T(8,128)(2,1)S(1)}, u32[]{:S(2)}, u32[]{:S(2)}) %all-to-all-start) | async-done | bytes 147488 | tf_op jit(solution)/shard_map/all_to_all | solution.py:23
  32.1 0.7 broadcast_in_dim.98
  32.8 13.9 %all-to-all-start.1 = ((bf16[64,8,256]{2,1,0:T(8,128)(2,1)}), bf16[64,8,256]{2,1,0:T(8,128)(2,1)S(1)}, u32[]{:S(2)}, u32[]{:S(2)}) async-start(bf16[64,8,256]{2,1,0:T(8,128)(2,1)} %broadcast_in_dim.98), calls=%async_computation.1 | async-start | bytes 524288 | tf_op jit(solution)/shard_map/all_to_all | solution.py:23
  47.5 13.0 %all-to-all-done.1 = bf16[64,8,256]{2,1,0:T(8,128)(2,1)S(1)} async-done(((bf16[64,8,256]{2,1,0:T(8,128)(2,1)}), bf16[64,8,256]{2,1,0:T(8,128)(2,1)S(1)}, u32[]{:S(2)}, u32[]{:S(2)}) %all-to-all-start.1) | async-done | bytes 262176 | tf_op jit(solution)/shard_map/all_to_all | solution.py:23
  60.5 3.6 %collective-permute-start = (bf16[64,8,256]{2,1,0:T(8,128)(2,1)S(1)}, bf16[64,8,256]{2,1,0:T(8,128)(2,1)S(1)}, u32[]{:S(2)}, u32[]{:S(2)}) collective-permute-start(bf16[64,8,256]{2,1,0:T(8,128)(2,1)S(1)} %all-to-all-done.1), channel_id=1, source_target_pairs={{0,1},{1,0},{2,3},{3,2},{4,5},{5,4},{6,7},{7,6},{8,9},{9,8},{10,11... | collective-permute-start | bytes 786440 | tf_op jit(solution)/shard_map/ppermute | solution.py:65
  64.4 0.9 collective-permute-done
  66.5 1.1 multiply_convert_fusion
  69.3 2.3 %collective-permute-start.1 = (bf16[64,8,384]{2,1,0:T(8,128)(2,1)S(1)}, bf16[64,8,384]{2,1,0:T(8,128)(2,1)S(1)}, u32[]{:S(2)}, u32[]{:S(2)}) collective-permute-start(bf16[64,8,384]{2,1,0:T(8,128)(2,1)S(1)} %pad_maximum_fusion.1), channel_id=1, source_target_pairs={{0,1},{1,0},{2,3},{3,2},{4,5},{5,4},{6,7},{7,6},{8,9},{9,8},{10,11... | collective-permute-start | bytes 1179656 | tf_op jit(solution)/shard_map/ppermute | solution.py:98
  71.6 1.3 %collective-permute-done.1 = bf16[64,8,384]{2,1,0:T(8,128)(2,1)S(1)} collective-permute-done((bf16[64,8,384]{2,1,0:T(8,128)(2,1)S(1)}, bf16[64,8,384]{2,1,0:T(8,128)(2,1)S(1)}, u32[]{:S(2)}, u32[]{:S(2)}) %collective-permute-start.1) | collective-permute-done | bytes 393248 | tf_op jit(solution)/shard_map/ppermute | solution.py:98
  72.9 0.8 add_convert_fusion
  73.8 4.6 %all-to-all-start.2 = ((bf16[64,8,384]{2,1,0:T(8,128)(2,1)}), bf16[64,8,384]{2,1,0:T(8,128)(2,1)S(1)}, u32[]{:S(2)}, u32[]{:S(2)}) async-start(bf16[64,8,384]{2,1,0:T(8,128)(2,1)} %add_convert_fusion), calls=%async_computation.2 | async-start | bytes 786432 | tf_op jit(solution)/shard_map/all_to_all | solution.py:23
  78.8 15.2 %all-to-all-done.2 = bf16[64,8,384]{2,1,0:T(8,128)(2,1)S(1)} async-done(((bf16[64,8,384]{2,1,0:T(8,128)(2,1)}), bf16[64,8,384]{2,1,0:T(8,128)(2,1)S(1)}, u32[]{:S(2)}, u32[]{:S(2)}) %all-to-all-start.2) | async-done | bytes 393248 | tf_op jit(solution)/shard_map/all_to_all | solution.py:23
  94.2 0.7 pad_maximum_fusion.2
  94.9 5.8 %all-to-all-start.3 = ((bf16[16,21,256]{2,1,0:T(8,128)(2,1)}), bf16[16,21,256]{2,1,0:T(8,128)(2,1)S(1)}, u32[]{:S(2)}, u32[]{:S(2)}) async-start(bf16[16,21,256]{2,1,0:T(8,128)(2,1)} %pad_maximum_fusion.2), calls=%async_computation.3 | async-start | bytes 393216 | tf_op jit(solution)/shard_map/all_to_all | solution.py:23
  101.1 10.0 %all-to-all-done.3 = bf16[16,21,256]{2,1,0:T(8,128)(2,1)S(1)} async-done(((bf16[16,21,256]{2,1,0:T(8,128)(2,1)}), bf16[16,21,256]{2,1,0:T(8,128)(2,1)S(1)}, u32[]{:S(2)}, u32[]{:S(2)}) %all-to-all-start.3) | async-done | bytes 172064 | tf_op jit(solution)/shard_map/all_to_all | solution.py:23
  111.2 0.7 broadcast_in_dim.105
  111.9 4.6 %all-to-all-start.4 = ((bf16[64,8,256]{2,1,0:T(8,128)(2,1)}), bf16[64,8,256]{2,1,0:T(8,128)(2,1)S(1)}, u32[]{:S(2)}, u32[]{:S(2)}) async-start(bf16[64,8,256]{2,1,0:T(8,128)(2,1)} %broadcast_in_dim.105), calls=%async_computation.4 | async-start | bytes 524288 | tf_op jit(solution)/shard_map/all_to_all | solution.py:23
  116.9 1.1 fusion.3
  118.0 12.6 %all-to-all-done.4 = bf16[64,8,256]{2,1,0:T(8,128)(2,1)S(1)} async-done(((bf16[64,8,256]{2,1,0:T(8,128)(2,1)}), bf16[64,8,256]{2,1,0:T(8,128)(2,1)S(1)}, u32[]{:S(2)}, u32[]{:S(2)}) %all-to-all-start.4) | async-done | bytes 262176 | tf_op jit(solution)/shard_map/all_to_all | solution.py:23
  130.6 0.8 slice_bitcast_fusion
  (69 shorter events, 7.1 us)
Async XLA Ops:
  0.6 1.7 %copy-start = (bf16[512,256]{1,0:T(8,128)(2,1)S(1)}, bf16[512,256]{1,0:T(8,128)(2,1)}, u32[]{:S(2)}) copy-start(bf16[512,256]{1,0:T(8,128)(2,1)} %param.10) | copy-start | bytes 786436
  0.6 21.0 %copy-start.5 = (bf16[256,256]{1,0:T(8,128)(2,1)S(1)}, bf16[256,256]{1,0:T(8,128)(2,1)}, u32[]{:S(2)}) copy-start(bf16[256,256]{1,0:T(8,128)(2,1)} %param.11) | copy-start | bytes 393220
  2.6 20.1 %copy-start.2 = (bf16[512,1024]{1,0:T(8,128)(2,1)S(1)}, bf16[512,1024]{1,0:T(8,128)(2,1)}, u32[]{:S(2)}) copy-start(bf16[512,1024]{1,0:T(8,128)(2,1)} %param.15) | copy-start | bytes 3145732
  4.2 27.8 %all-to-all-start = ((bf16[16,18,256]{2,1,0:T(8,128)(2,1)}), bf16[16,18,256]{2,1,0:T(8,128)(2,1)S(1)}, u32[]{:S(2)}, u32[]{:S(2)}) async-start(bf16[16,18,256]{2,1,0:T(8,128)(2,1)} %broadcast_select_fusion.5), calls=%async_computation | async-start | bytes 393216 | tf_op jit(solution)/shard_map/all_to_all | solution.py:23
  21.7 1.3 copy-start.1
  22.9 24.5 %copy-start.3 = (bf16[512,256]{1,0:T(8,128)(2,1)S(1)}, bf16[512,256]{1,0:T(8,128)(2,1)}, u32[]{:S(2)}) copy-start(bf16[512,256]{1,0:T(8,128)(2,1)} %param.18) | copy-start | bytes 786436
  32.8 27.8 %all-to-all-start.1 = ((bf16[64,8,256]{2,1,0:T(8,128)(2,1)}), bf16[64,8,256]{2,1,0:T(8,128)(2,1)S(1)}, u32[]{:S(2)}, u32[]{:S(2)}) async-start(bf16[64,8,256]{2,1,0:T(8,128)(2,1)} %broadcast_in_dim.98), calls=%async_computation.1 | async-start | bytes 524288 | tf_op jit(solution)/shard_map/all_to_all | solution.py:23
  60.5 4.8 %collective-permute-start = (bf16[64,8,256]{2,1,0:T(8,128)(2,1)S(1)}, bf16[64,8,256]{2,1,0:T(8,128)(2,1)S(1)}, u32[]{:S(2)}, u32[]{:S(2)}) collective-permute-start(bf16[64,8,256]{2,1,0:T(8,128)(2,1)S(1)} %all-to-all-done.1), channel_id=1, source_target_pairs={{0,1},{1,0},{2,3},{3,2},{4,5},{5,4},{6,7},{7,6},{8,9},{9,8},{10,11... | collective-permute-start | bytes 786440 | tf_op jit(solution)/shard_map/ppermute | solution.py:65
  65.4 1.0 copy-start.4
  65.4 1.1 copy-start.7
  65.4 1.1 copy-start.8
  69.3 9.1 %copy-start.6 = (s32[1,16,16]{2,1,0:T(8,128)S(1)}, s32[1,16,16]{2,1,0:T(8,128)}, u32[]{:S(2)}) copy-start(s32[1,16,16]{2,1,0:T(8,128)} %param.16) | copy-start | bytes 3076
  69.3 3.6 %collective-permute-start.1 = (bf16[64,8,384]{2,1,0:T(8,128)(2,1)S(1)}, bf16[64,8,384]{2,1,0:T(8,128)(2,1)S(1)}, u32[]{:S(2)}, u32[]{:S(2)}) collective-permute-start(bf16[64,8,384]{2,1,0:T(8,128)(2,1)S(1)} %pad_maximum_fusion.1), channel_id=1, source_target_pairs={{0,1},{1,0},{2,3},{3,2},{4,5},{5,4},{6,7},{7,6},{8,9},{9,8},{10,11... | collective-permute-start | bytes 1179656 | tf_op jit(solution)/shard_map/ppermute | solution.py:98
  73.8 20.2 %all-to-all-start.2 = ((bf16[64,8,384]{2,1,0:T(8,128)(2,1)}), bf16[64,8,384]{2,1,0:T(8,128)(2,1)S(1)}, u32[]{:S(2)}, u32[]{:S(2)}) async-start(bf16[64,8,384]{2,1,0:T(8,128)(2,1)} %add_convert_fusion), calls=%async_computation.2 | async-start | bytes 786432 | tf_op jit(solution)/shard_map/all_to_all | solution.py:23
  94.9 16.2 %all-to-all-start.3 = ((bf16[16,21,256]{2,1,0:T(8,128)(2,1)}), bf16[16,21,256]{2,1,0:T(8,128)(2,1)S(1)}, u32[]{:S(2)}, u32[]{:S(2)}) async-start(bf16[16,21,256]{2,1,0:T(8,128)(2,1)} %pad_maximum_fusion.2), calls=%async_computation.3 | async-start | bytes 393216 | tf_op jit(solution)/shard_map/all_to_all | solution.py:23
  111.9 18.6 %all-to-all-start.4 = ((bf16[64,8,256]{2,1,0:T(8,128)(2,1)}), bf16[64,8,256]{2,1,0:T(8,128)(2,1)S(1)}, u32[]{:S(2)}, u32[]{:S(2)}) async-start(bf16[64,8,256]{2,1,0:T(8,128)(2,1)} %broadcast_in_dim.105), calls=%async_computation.4 | async-start | bytes 524288 | tf_op jit(solution)/shard_map/all_to_all | solution.py:23

commit v3 on v2

--- a/solution.py
+++ b/solution.py
@@ -1,6 +1,8 @@
 import jax
 import jax.numpy as jnp
 from jax import lax
+from jax.experimental import pallas as pl
+from jax.experimental.pallas import tpu as pltpu
 from jax.sharding import PartitionSpec as P
 
 F32 = jnp.float32
@@ -23,6 +25,34 @@
     return lax.all_to_all(x, axis, split_axis=0, concat_axis=0, tiled=True)
 
 
+def pack_kernel(features_ref, rows_ref, hub_ref, count_ref, message_ref):
+    nodes, feat = features_ref.shape
+    peers, slots = rows_ref.shape[1:]
+    listed = rows_ref[0]
+    wanted = jnp.concatenate([listed[p : p + 1] for p in range(peers)], axis=1)
+    row_ids = lax.broadcasted_iota(jnp.int32, (nodes, peers * slots), 0)
+    picked = dot_t((row_ids == wanted).astype(BF16), features_ref[...])
+    hub_ids = lax.broadcasted_iota(jnp.int32, (8, nodes), 1)
+    hub = dot((hub_ids == hub_ref[0, 0]).astype(BF16), features_ref[...])[:1]
+    for p in range(peers):
+        count = jnp.full((1, feat), count_ref[0, p].astype(F32))
+        rows = picked[p * slots : (p + 1) * slots]
+        message_ref[p] = jnp.concatenate([rows, hub, count], axis=0).astype(BF16)
+
+
+def pack(features, send_rows, hub_rows, send_count):
+    feat = features.shape[1]
+    peers, slots = send_rows.shape[1:]
+    vmem = pl.BlockSpec(memory_space=pltpu.VMEM)
+    smem = pl.BlockSpec(memory_space=pltpu.SMEM)
+    return pl.pallas_call(
+        pack_kernel,
+        out_shape=jax.ShapeDtypeStruct((peers, slots + 2, feat), BF16),
+        in_specs=[vmem, vmem, smem, smem],
+        out_specs=vmem,
+    )(features, send_rows, hub_rows, send_count)
+
+
 def per_device(
     features,
     w_self,
@@ -41,18 +71,7 @@
     hubs = hub_weight.shape[1]
     row_ids = jnp.arange(nodes, dtype=jnp.int32)
 
-    pick = jnp.concatenate(
-        [
-            send_rows[0],
-            jnp.broadcast_to(hub_rows, (peers, 1)),
-            jnp.full((peers, 1), -1, jnp.int32),
-        ],
-        axis=1,
-    )
-    pick_hot = (pick[:, :, None] == row_ids).astype(BF16).reshape(-1, nodes)
-    message = dot(pick_hot, features).astype(BF16).reshape(peers, slots + 2, feat)
-    count_slot = (jnp.arange(slots + 2) == slots + 1)[None, :, None]
-    message = jnp.where(count_slot, send_count[0].astype(BF16)[:, None, None], message)
+    message = pack(features, send_rows, hub_rows, send_count)
     got = exchange(message, "col")
     halo_feat = got[:, :slots].reshape(peers * slots, feat)
     group_hubs = got[:, slots]
@@ -77,7 +96,12 @@
     )[:, None]
     agg_sum = dot(local_weight, features) + dot(halo_used, halo_feat) + dot(hub_weight, hub_feat)
     neigh = (agg_sum / degree).astype(BF16)
-    preact = dot(features, w_self) + dot(neigh, w_neigh)
+    preact = lax.dot_general(
+        jnp.stack([features, neigh]),
+        jnp.stack([w_self, w_neigh]),
+        (((0, 2), (0, 1)), ((), ())),
+        preferred_element_type=F32,
+    )
     sig = jax.nn.sigmoid(preact)
     output = (preact * sig).astype(BF16)
     grad_pre = (grad_out.astype(F32) * (sig + preact * sig * (1.0 - sig))).astype(BF16)

time: 132 us -> 131 us (level)
  Pallas kernels: 0 us -> 2.02 us
  matrix products: 6.63 us -> 5.3 us
    dot_general x6 -> x3, matrix products: 3.38 us -> 0.96 us  [dot(): return jnp.dot(a, b, preferred_element_type=F32)]
    pallas_call x0 -> x1, Pallas kernels: none -> 2.02 us  [pack(): pl.pallas_call(pack_kernel, out_shape=jax.ShapeDtypeStruct((peers, slots...]
where the time goes in v3:
time: 131 us
  waiting for transfers between devices  62 us (47%)
  starting transfers between devices  51.6 us (39%)
  matrix products  5.3 us (4%)
  other arithmetic  4.3 us (3%)
  local copies, waits for them, and re-layouts  3.6 us (3%)
  Pallas kernels  2.02 us (2%)
  between operations  1.69 us (1%)
    all_to_all x5, waiting for transfers between devices, exchange(): return lax.all_to_all(x, axis, split_axis=0, concat_axis=0, tiled=True)  59.6 us
    all_to_all x5, starting transfers between devices, exchange(): return lax.all_to_all(x, axis, split_axis=0, concat_axis=0, tiled=True)  46 us
    ppermute x1, starting transfers between devices, per_device(): other = lax.ppermute(held, 'col', swap)  3.61 us
    dot_general x6, matrix products, dot_t(): lax.dot_general(a, b, (((0,), (0,)), ((), ())), preferred_element_type=F32)  2.72 us
  transfers between devices with their start and end apart: 7, of which 7 were waited for; matrix products, arithmetic and copies ran while one was open for 4% of the time, Pallas kernels for 0%

profile of v3, /device:TPU:1, one launch (start us, length us, event | category | flops | bytes accessed | tf_op | source)
XLA Modules:
  0.0 130.6 jit_solution(15523959123593151874)
XLA Ops:
  1.4 2.0 %shard_map.129 = bf16[16,18,256]{2,1,0:T(8,128)(2,1)} custom-call(bf16[512,256]{1,0:T(8,128)(2,1)} %features_ref.1, s32[1,16,16]{2,1,0:T(8,128)} %rows_ref.1, s32[1,1]{1,0:T(1,128)} %copy.30.hub_ref, s32[1,16]{1,0:T(1,128)} %count_ref.1), custom_call_target="tpu_custom_call" | custom-call | tf_op jit(solution)/shard_map/pallas_call | solution.py:48
  3.4 17.5 %all-to-all-start = ((bf16[16,18,256]{2,1,0:T(8,128)(2,1)}), bf16[16,18,256]{2,1,0:T(8,128)(2,1)S(1)}, u32[]{:S(2)}, u32[]{:S(2)}) async-start(bf16[16,18,256]{2,1,0:T(8,128)(2,1)} %shard_map.129), calls=%async_computation | async-start | bytes 393216 | tf_op jit(solution)/shard_map/all_to_all | solution.py:25
  20.9 1.4 %convert_reduce_fusion = f32[512]{0:T(512)S(1)} fusion(bf16[512,1024]{1,0:T(8,128)(2,1)} %param.15), kind=kLoop, calls=%fused_computation | loop fusion | flops 1048064 | bytes 1050624 | tf_op jit(solution)/shard_map/reduce_sum | solution.py:94
  22.6 8.6 %all-to-all-done = bf16[16,18,256]{2,1,0:T(8,128)(2,1)S(1)} async-done(((bf16[16,18,256]{2,1,0:T(8,128)(2,1)}), bf16[16,18,256]{2,1,0:T(8,128)(2,1)S(1)}, u32[]{:S(2)}, u32[]{:S(2)}) %all-to-all-start) | async-done | bytes 147488 | tf_op jit(solution)/shard_map/all_to_all | solution.py:25
  31.3 0.7 broadcast_in_dim.67
  32.0 13.9 %all-to-all-start.1 = ((bf16[64,8,256]{2,1,0:T(8,128)(2,1)}), bf16[64,8,256]{2,1,0:T(8,128)(2,1)S(1)}, u32[]{:S(2)}, u32[]{:S(2)}) async-start(bf16[64,8,256]{2,1,0:T(8,128)(2,1)} %broadcast_in_dim.67), calls=%async_computation.1 | async-start | bytes 524288 | tf_op jit(solution)/shard_map/all_to_all | solution.py:25
  46.7 13.0 %all-to-all-done.1 = bf16[64,8,256]{2,1,0:T(8,128)(2,1)S(1)} async-done(((bf16[64,8,256]{2,1,0:T(8,128)(2,1)}), bf16[64,8,256]{2,1,0:T(8,128)(2,1)S(1)}, u32[]{:S(2)}, u32[]{:S(2)}) %all-to-all-start.1) | async-done | bytes 262176 | tf_op jit(solution)/shard_map/all_to_all | solution.py:25
  59.7 3.6 %collective-permute-start = (bf16[64,8,256]{2,1,0:T(8,128)(2,1)S(1)}, bf16[64,8,256]{2,1,0:T(8,128)(2,1)S(1)}, u32[]{:S(2)}, u32[]{:S(2)}) collective-permute-start(bf16[64,8,256]{2,1,0:T(8,128)(2,1)S(1)} %all-to-all-done.1), channel_id=1, source_target_pairs={{0,1},{1,0},{2,3},{3,2},{4,5},{5,4},{6,7},{7,6},{8,9},{9,8},{10,11... | collective-permute-start | bytes 786440 | tf_op jit(solution)/shard_map/ppermute | solution.py:84
  63.6 0.9 collective-permute-done
  65.9 1.1 multiply_convert_fusion
  67.8 0.5 convolution_bitcast_fusion
  68.7 2.1 %collective-permute-start.1 = (bf16[64,8,384]{2,1,0:T(8,128)(2,1)S(1)}, bf16[64,8,384]{2,1,0:T(8,128)(2,1)S(1)}, u32[]{:S(2)}, u32[]{:S(2)}) collective-permute-start(bf16[64,8,384]{2,1,0:T(8,128)(2,1)S(1)} %pad_maximum_fusion.1), channel_id=1, source_target_pairs={{0,1},{1,0},{2,3},{3,2},{4,5},{5,4},{6,7},{7,6},{8,9},{9,8},{10,11... | collective-permute-start | bytes 1179656 | tf_op jit(solution)/shard_map/ppermute | solution.py:122
  70.7 1.6 %collective-permute-done.1 = bf16[64,8,384]{2,1,0:T(8,128)(2,1)S(1)} collective-permute-done((bf16[64,8,384]{2,1,0:T(8,128)(2,1)S(1)}, bf16[64,8,384]{2,1,0:T(8,128)(2,1)S(1)}, u32[]{:S(2)}, u32[]{:S(2)}) %collective-permute-start.1) | collective-permute-done | bytes 393248 | tf_op jit(solution)/shard_map/ppermute | solution.py:122
  72.3 0.9 add_convert_fusion
  73.1 4.6 %all-to-all-start.2 = ((bf16[64,8,384]{2,1,0:T(8,128)(2,1)}), bf16[64,8,384]{2,1,0:T(8,128)(2,1)S(1)}, u32[]{:S(2)}, u32[]{:S(2)}) async-start(bf16[64,8,384]{2,1,0:T(8,128)(2,1)} %add_convert_fusion), calls=%async_computation.2 | async-start | bytes 786432 | tf_op jit(solution)/shard_map/all_to_all | solution.py:25
  78.2 15.5 %all-to-all-done.2 = bf16[64,8,384]{2,1,0:T(8,128)(2,1)S(1)} async-done(((bf16[64,8,384]{2,1,0:T(8,128)(2,1)}), bf16[64,8,384]{2,1,0:T(8,128)(2,1)S(1)}, u32[]{:S(2)}, u32[]{:S(2)}) %all-to-all-start.2) | async-done | bytes 393248 | tf_op jit(solution)/shard_map/all_to_all | solution.py:25
  93.9 0.7 pad_maximum_fusion.2
  94.6 5.0 %all-to-all-start.3 = ((bf16[16,21,256]{2,1,0:T(8,128)(2,1)}), bf16[16,21,256]{2,1,0:T(8,128)(2,1)S(1)}, u32[]{:S(2)}, u32[]{:S(2)}) async-start(bf16[16,21,256]{2,1,0:T(8,128)(2,1)} %pad_maximum_fusion.2), calls=%async_computation.3 | async-start | bytes 393216 | tf_op jit(solution)/shard_map/all_to_all | solution.py:25
  99.9 10.0 %all-to-all-done.3 = bf16[16,21,256]{2,1,0:T(8,128)(2,1)S(1)} async-done(((bf16[16,21,256]{2,1,0:T(8,128)(2,1)}), bf16[16,21,256]{2,1,0:T(8,128)(2,1)S(1)}, u32[]{:S(2)}, u32[]{:S(2)}) %all-to-all-start.3) | async-done | bytes 172064 | tf_op jit(solution)/shard_map/all_to_all | solution.py:25
  110.0 0.7 broadcast_in_dim.74
  110.7 5.0 %all-to-all-start.4 = ((bf16[64,8,256]{2,1,0:T(8,128)(2,1)}), bf16[64,8,256]{2,1,0:T(8,128)(2,1)S(1)}, u32[]{:S(2)}, u32[]{:S(2)}) async-start(bf16[64,8,256]{2,1,0:T(8,128)(2,1)} %broadcast_in_dim.74), calls=%async_computation.4 | async-start | bytes 524288 | tf_op jit(solution)/shard_map/all_to_all | solution.py:25
  116.1 1.1 fusion.3
  117.2 12.5 %all-to-all-done.4 = bf16[64,8,256]{2,1,0:T(8,128)(2,1)S(1)} async-done(((bf16[64,8,256]{2,1,0:T(8,128)(2,1)}), bf16[64,8,256]{2,1,0:T(8,128)(2,1)S(1)}, u32[]{:S(2)}, u32[]{:S(2)}) %all-to-all-start.4) | async-done | bytes 262176 | tf_op jit(solution)/shard_map/all_to_all | solution.py:25
  129.8 0.8 slice_bitcast_fusion
  (58 shorter events, 5.3 us)
Async XLA Ops:
  0.6 21.7 %copy-start.2 = (bf16[512,256]{1,0:T(8,128)(2,1)S(1)}, bf16[512,256]{1,0:T(8,128)(2,1)}, u32[]{:S(2)}) copy-start(bf16[512,256]{1,0:T(8,128)(2,1)} %features_ref.1) | copy-start | bytes 786436
  0.6 21.7 %copy-start = (bf16[512,512]{1,0:T(8,128)(2,1)S(1)}, bf16[512,512]{1,0:T(8,128)(2,1)}, u32[]{:S(2)}) copy-start(bf16[512,512]{1,0:T(8,128)(2,1)} %param.13) | copy-start | bytes 1572868
  3.4 27.8 %all-to-all-start = ((bf16[16,18,256]{2,1,0:T(8,128)(2,1)}), bf16[16,18,256]{2,1,0:T(8,128)(2,1)S(1)}, u32[]{:S(2)}, u32[]{:S(2)}) async-start(bf16[16,18,256]{2,1,0:T(8,128)(2,1)} %shard_map.129), calls=%async_computation | async-start | bytes 393216 | tf_op jit(solution)/shard_map/all_to_all | solution.py:25
  22.3 24.3 %copy-start.3 = (bf16[512,256]{1,0:T(8,128)(2,1)S(1)}, bf16[512,256]{1,0:T(8,128)(2,1)}, u32[]{:S(2)}) copy-start(bf16[512,256]{1,0:T(8,128)(2,1)} %param.18) | copy-start | bytes 786436
  32.0 27.8 %all-to-all-start.1 = ((bf16[64,8,256]{2,1,0:T(8,128)(2,1)}), bf16[64,8,256]{2,1,0:T(8,128)(2,1)S(1)}, u32[]{:S(2)}, u32[]{:S(2)}) async-start(bf16[64,8,256]{2,1,0:T(8,128)(2,1)} %broadcast_in_dim.67), calls=%async_computation.1 | async-start | bytes 524288 | tf_op jit(solution)/shard_map/all_to_all | solution.py:25
  59.7 4.8 %collective-permute-start = (bf16[64,8,256]{2,1,0:T(8,128)(2,1)S(1)}, bf16[64,8,256]{2,1,0:T(8,128)(2,1)S(1)}, u32[]{:S(2)}, u32[]{:S(2)}) collective-permute-start(bf16[64,8,256]{2,1,0:T(8,128)(2,1)S(1)} %all-to-all-done.1), channel_id=1, source_target_pairs={{0,1},{1,0},{2,3},{3,2},{4,5},{5,4},{6,7},{7,6},{8,9},{9,8},{10,11... | collective-permute-start | bytes 786440 | tf_op jit(solution)/shard_map/ppermute | solution.py:84
  63.6 1.2 copy-start.1
  64.9 0.9 copy-start.4
  64.9 1.0 copy-start.6
  64.9 1.0 copy-start.7
  68.7 9.1 %copy-start.5 = (s32[1,16,16]{2,1,0:T(8,128)S(1)}, s32[1,16,16]{2,1,0:T(8,128)}, u32[]{:S(2)}) copy-start(s32[1,16,16]{2,1,0:T(8,128)} %rows_ref.1) | copy-start | bytes 3076
  68.7 3.6 %collective-permute-start.1 = (bf16[64,8,384]{2,1,0:T(8,128)(2,1)S(1)}, bf16[64,8,384]{2,1,0:T(8,128)(2,1)S(1)}, u32[]{:S(2)}, u32[]{:S(2)}) collective-permute-start(bf16[64,8,384]{2,1,0:T(8,128)(2,1)S(1)} %pad_maximum_fusion.1), channel_id=1, source_target_pairs={{0,1},{1,0},{2,3},{3,2},{4,5},{5,4},{6,7},{7,6},{8,9},{9,8},{10,11... | collective-permute-start | bytes 1179656 | tf_op jit(solution)/shard_map/ppermute | solution.py:122
  73.1 20.5 %all-to-all-start.2 = ((bf16[64,8,384]{2,1,0:T(8,128)(2,1)}), bf16[64,8,384]{2,1,0:T(8,128)(2,1)S(1)}, u32[]{:S(2)}, u32[]{:S(2)}) async-start(bf16[64,8,384]{2,1,0:T(8,128)(2,1)} %add_convert_fusion), calls=%async_computation.2 | async-start | bytes 786432 | tf_op jit(solution)/shard_map/all_to_all | solution.py:25
  94.6 15.4 %all-to-all-start.3 = ((bf16[16,21,256]{2,1,0:T(8,128)(2,1)}), bf16[16,21,256]{2,1,0:T(8,128)(2,1)S(1)}, u32[]{:S(2)}, u32[]{:S(2)}) async-start(bf16[16,21,256]{2,1,0:T(8,128)(2,1)} %pad_maximum_fusion.2), calls=%async_computation.3 | async-start | bytes 393216 | tf_op jit(solution)/shard_map/all_to_all | solution.py:25
  110.7 19.0 %all-to-all-start.4 = ((bf16[64,8,256]{2,1,0:T(8,128)(2,1)}), bf16[64,8,256]{2,1,0:T(8,128)(2,1)S(1)}, u32[]{:S(2)}, u32[]{:S(2)}) async-start(bf16[64,8,256]{2,1,0:T(8,128)(2,1)} %broadcast_in_dim.74), calls=%async_computation.4 | async-start | bytes 524288 | tf_op jit(solution)/shard_map/all_to_all | solution.py:25

commit v4 on v3

--- a/solution.py
+++ b/solution.py
@@ -88,6 +88,9 @@
 
     live = (jnp.arange(slots, dtype=jnp.int32)[None, :] < counts[:, None]).reshape(-1)
     halo_used = jnp.where(live[None, :], halo_weight, jnp.zeros((), BF16))
+    w_both, hub_weight_t = lax.optimization_barrier(
+        (jnp.stack([w_self, w_neigh]), hub_weight.T)
+    )
     degree = (
         1.0
         + jnp.sum(local_weight.astype(F32), axis=1)
@@ -98,20 +101,24 @@
     neigh = (agg_sum / degree).astype(BF16)
     preact = lax.dot_general(
         jnp.stack([features, neigh]),
-        jnp.stack([w_self, w_neigh]),
+        w_both,
         (((0, 2), (0, 1)), ((), ())),
         preferred_element_type=F32,
     )
     sig = jax.nn.sigmoid(preact)
     output = (preact * sig).astype(BF16)
     grad_pre = (grad_out.astype(F32) * (sig + preact * sig * (1.0 - sig))).astype(BF16)
-    part_self = dot_t(features, grad_pre)
-    part_neigh = dot_t(neigh, grad_pre)
+    parts = lax.dot_general(
+        jnp.stack([features, neigh]),
+        grad_pre,
+        (((1,), (0,)), ((), ())),
+        preferred_element_type=F32,
+    )
     grad_agg = (dot_nt(grad_pre, w_neigh) / degree).astype(BF16)
-    hub_partial = dot_t(hub_weight, grad_agg)
+    hub_partial = dot(hub_weight_t, grad_agg)
 
     hub_halves = hub_partial.reshape(groups, 2, half, feat)
-    weights = jnp.concatenate([part_self, part_neigh], axis=0).reshape(groups, -1, feat)
+    weights = parts.reshape(groups, -1, feat)
     share = weights.shape[1]
 
     def piece(which):

time: 131 us -> 131 us (level)
    dot_general x6 -> x3, matrix products: 2.72 us -> 1.72 us  [dot_t(): lax.dot_general(a, b, (((0,), (0,)), ((), ())), preferred_element_type=F32)]
where the time goes in v4:
time: 131 us; the launch traced here: 130 us
  waiting for transfers between devices  61.9 us (47%)
  starting transfers between devices  51.8 us (40%)
  matrix products  5.15 us (4%)
  other arithmetic  4.32 us (3%)
  local copies, waits for them, and re-layouts  3.32 us (3%)
  Pallas kernels  2.02 us (2%)
  between operations  1.7 us (1%)
    all_to_all x5, waiting for transfers between devices, exchange(): return lax.all_to_all(x, axis, split_axis=0, concat_axis=0, tiled=True)  59.6 us
    all_to_all x5, starting transfers between devices, exchange(): return lax.all_to_all(x, axis, split_axis=0, concat_axis=0, tiled=True)  46.1 us
    ppermute x1, starting transfers between devices, per_device(): other = lax.ppermute(held, 'col', swap)  3.61 us
  transfers between devices with their start and end apart: 7, of which 7 were waited for; matrix products, arithmetic and copies ran while one was open for 4% of the time, Pallas kernels for 0%

profile of v4, /device:TPU:1, one launch (start us, length us, event | category | flops | bytes accessed | tf_op | source)
XLA Modules:
  0.0 130.2 jit_solution(14642953708251645367)
XLA Ops:
  1.3 2.0 %shard_map.129 = bf16[16,18,256]{2,1,0:T(8,128)(2,1)} custom-call(bf16[512,256]{1,0:T(8,128)(2,1)} %features_ref.1, s32[1,16,16]{2,1,0:T(8,128)} %rows_ref.1, s32[1,1]{1,0:T(1,128)} %copy.34.hub_ref, s32[1,16]{1,0:T(1,128)} %count_ref.1), custom_call_target="tpu_custom_call" | custom-call | tf_op jit(solution)/shard_map/pallas_call | solution.py:48
  3.4 17.6 %all-to-all-start = ((bf16[16,18,256]{2,1,0:T(8,128)(2,1)}), bf16[16,18,256]{2,1,0:T(8,128)(2,1)S(1)}, u32[]{:S(2)}, u32[]{:S(2)}) async-start(bf16[16,18,256]{2,1,0:T(8,128)(2,1)} %shard_map.129), calls=%async_computation | async-start | bytes 393216 | tf_op jit(solution)/shard_map/all_to_all | solution.py:25
  21.0 1.4 %convert_reduce_fusion = f32[512]{0:T(512)S(1)} fusion(bf16[512,1024]{1,0:T(8,128)(2,1)} %param.15), kind=kLoop, calls=%fused_computation | loop fusion | flops 1048064 | bytes 1050624 | tf_op jit(solution)/shard_map/reduce_sum | solution.py:97
  22.9 8.4 %all-to-all-done = bf16[16,18,256]{2,1,0:T(8,128)(2,1)S(1)} async-done(((bf16[16,18,256]{2,1,0:T(8,128)(2,1)}), bf16[16,18,256]{2,1,0:T(8,128)(2,1)S(1)}, u32[]{:S(2)}, u32[]{:S(2)}) %all-to-all-start) | async-done | bytes 147488 | tf_op jit(solution)/shard_map/all_to_all | solution.py:25
  31.4 0.7 broadcast_in_dim.67
  32.1 13.9 %all-to-all-start.1 = ((bf16[64,8,256]{2,1,0:T(8,128)(2,1)}), bf16[64,8,256]{2,1,0:T(8,128)(2,1)S(1)}, u32[]{:S(2)}, u32[]{:S(2)}) async-start(bf16[64,8,256]{2,1,0:T(8,128)(2,1)} %broadcast_in_dim.67), calls=%async_computation.1 | async-start | bytes 524288 | tf_op jit(solution)/shard_map/all_to_all | solution.py:25
  46.8 13.1 %all-to-all-done.1 = bf16[64,8,256]{2,1,0:T(8,128)(2,1)S(1)} async-done(((bf16[64,8,256]{2,1,0:T(8,128)(2,1)}), bf16[64,8,256]{2,1,0:T(8,128)(2,1)S(1)}, u32[]{:S(2)}, u32[]{:S(2)}) %all-to-all-start.1) | async-done | bytes 262176 | tf_op jit(solution)/shard_map/all_to_all | solution.py:25
  59.9 3.6 %collective-permute-start = (bf16[64,8,256]{2,1,0:T(8,128)(2,1)S(1)}, bf16[64,8,256]{2,1,0:T(8,128)(2,1)S(1)}, u32[]{:S(2)}, u32[]{:S(2)}) collective-permute-start(bf16[64,8,256]{2,1,0:T(8,128)(2,1)S(1)} %all-to-all-done.1), channel_id=1, source_target_pairs={{0,1},{1,0},{2,3},{3,2},{4,5},{5,4},{6,7},{7,6},{8,9},{9,8},{10,11... | collective-permute-start | bytes 786440 | tf_op jit(solution)/shard_map/ppermute | solution.py:84
  63.8 0.9 collective-permute-done
  65.4 0.5 copy-done.7
  65.9 1.1 multiply_convert_fusion
  68.3 2.0 %collective-permute-start.1 = (bf16[64,8,384]{2,1,0:T(8,128)(2,1)S(1)}, bf16[64,8,384]{2,1,0:T(8,128)(2,1)S(1)}, u32[]{:S(2)}, u32[]{:S(2)}) collective-permute-start(bf16[64,8,384]{2,1,0:T(8,128)(2,1)S(1)} %pad_maximum_fusion.2), channel_id=1, source_target_pairs={{0,1},{1,0},{2,3},{3,2},{4,5},{5,4},{6,7},{7,6},{8,9},{9,8},{10,11... | collective-permute-start | bytes 1179656 | tf_op jit(solution)/shard_map/ppermute | solution.py:129
  70.4 1.5 %collective-permute-done.1 = bf16[64,8,384]{2,1,0:T(8,128)(2,1)S(1)} collective-permute-done((bf16[64,8,384]{2,1,0:T(8,128)(2,1)S(1)}, bf16[64,8,384]{2,1,0:T(8,128)(2,1)S(1)}, u32[]{:S(2)}, u32[]{:S(2)}) %collective-permute-start.1) | collective-permute-done | bytes 393248 | tf_op jit(solution)/shard_map/ppermute | solution.py:129
  71.9 0.9 add_convert_fusion
  72.7 4.6 %all-to-all-start.2 = ((bf16[64,8,384]{2,1,0:T(8,128)(2,1)}), bf16[64,8,384]{2,1,0:T(8,128)(2,1)S(1)}, u32[]{:S(2)}, u32[]{:S(2)}) async-start(bf16[64,8,384]{2,1,0:T(8,128)(2,1)} %add_convert_fusion), calls=%async_computation.2 | async-start | bytes 786432 | tf_op jit(solution)/shard_map/all_to_all | solution.py:25
  77.8 15.5 %all-to-all-done.2 = bf16[64,8,384]{2,1,0:T(8,128)(2,1)S(1)} async-done(((bf16[64,8,384]{2,1,0:T(8,128)(2,1)}), bf16[64,8,384]{2,1,0:T(8,128)(2,1)S(1)}, u32[]{:S(2)}, u32[]{:S(2)}) %all-to-all-start.2) | async-done | bytes 393248 | tf_op jit(solution)/shard_map/all_to_all | solution.py:25
  93.5 0.7 pad_maximum_fusion.6
  94.2 4.9 %all-to-all-start.3 = ((bf16[16,21,256]{2,1,0:T(8,128)(2,1)}), bf16[16,21,256]{2,1,0:T(8,128)(2,1)S(1)}, u32[]{:S(2)}, u32[]{:S(2)}) async-start(bf16[16,21,256]{2,1,0:T(8,128)(2,1)} %pad_maximum_fusion.6), calls=%async_computation.3 | async-start | bytes 393216 | tf_op jit(solution)/shard_map/all_to_all | solution.py:25
  99.5 10.0 %all-to-all-done.3 = bf16[16,21,256]{2,1,0:T(8,128)(2,1)S(1)} async-done(((bf16[16,21,256]{2,1,0:T(8,128)(2,1)}), bf16[16,21,256]{2,1,0:T(8,128)(2,1)S(1)}, u32[]{:S(2)}, u32[]{:S(2)}) %all-to-all-start.3) | async-done | bytes 172064 | tf_op jit(solution)/shard_map/all_to_all | solution.py:25
  109.6 0.7 broadcast_in_dim.74
  110.3 5.0 %all-to-all-start.4 = ((bf16[64,8,256]{2,1,0:T(8,128)(2,1)}), bf16[64,8,256]{2,1,0:T(8,128)(2,1)S(1)}, u32[]{:S(2)}, u32[]{:S(2)}) async-start(bf16[64,8,256]{2,1,0:T(8,128)(2,1)} %broadcast_in_dim.74), calls=%async_computation.4 | async-start | bytes 524288 | tf_op jit(solution)/shard_map/all_to_all | solution.py:25
  115.7 1.1 fusion.3
  116.8 12.5 %all-to-all-done.4 = bf16[64,8,256]{2,1,0:T(8,128)(2,1)S(1)} async-done(((bf16[64,8,256]{2,1,0:T(8,128)(2,1)}), bf16[64,8,256]{2,1,0:T(8,128)(2,1)S(1)}, u32[]{:S(2)}, u32[]{:S(2)}) %all-to-all-start.4) | async-done | bytes 262176 | tf_op jit(solution)/shard_map/all_to_all | solution.py:25
  129.4 0.8 slice_bitcast_fusion
  (57 shorter events, 4.8 us)
Async XLA Ops:
  0.6 21.8 %copy-start = (bf16[512,512]{1,0:T(8,128)(2,1)S(1)}, bf16[512,512]{1,0:T(8,128)(2,1)}, u32[]{:S(2)}) copy-start(bf16[512,512]{1,0:T(8,128)(2,1)} %param.13) | copy-start | bytes 1572868
  3.4 19.2 %copy-start.1 = (bf16[512,256]{1,0:T(8,128)(2,1)S(1)}, bf16[512,256]{1,0:T(8,128)(2,1)}, u32[]{:S(2)}) copy-start(bf16[512,256]{1,0:T(8,128)(2,1)} %features_ref.1) | copy-start | bytes 786436
  3.4 28.0 %all-to-all-start = ((bf16[16,18,256]{2,1,0:T(8,128)(2,1)}), bf16[16,18,256]{2,1,0:T(8,128)(2,1)S(1)}, u32[]{:S(2)}, u32[]{:S(2)}) async-start(bf16[16,18,256]{2,1,0:T(8,128)(2,1)} %shard_map.129), calls=%async_computation | async-start | bytes 393216 | tf_op jit(solution)/shard_map/all_to_all | solution.py:25
  22.6 23.4 %copy-start.4 = (bf16[256,256]{1,0:T(8,128)(2,1)S(1)}, bf16[256,256]{1,0:T(8,128)(2,1)}, u32[]{:S(2)}) copy-start(bf16[256,256]{1,0:T(8,128)(2,1)} %param.11) | copy-start | bytes 393220
  22.6 23.4 %copy-start.5 = (bf16[256,256]{1,0:T(8,128)(2,1)S(1)}, bf16[256,256]{1,0:T(8,128)(2,1)}, u32[]{:S(2)}) copy-start(bf16[256,256]{1,0:T(8,128)(2,1)} %param.12) | copy-start | bytes 393220
  22.6 24.0 %copy-start.3 = (bf16[512,256]{1,0:T(8,128)(2,1)S(1)}, bf16[512,256]{1,0:T(8,128)(2,1)}, u32[]{:S(2)}) copy-start(bf16[512,256]{1,0:T(8,128)(2,1)} %param.18) | copy-start | bytes 786436
  32.1 27.8 %all-to-all-start.1 = ((bf16[64,8,256]{2,1,0:T(8,128)(2,1)}), bf16[64,8,256]{2,1,0:T(8,128)(2,1)S(1)}, u32[]{:S(2)}, u32[]{:S(2)}) async-start(bf16[64,8,256]{2,1,0:T(8,128)(2,1)} %broadcast_in_dim.67), calls=%async_computation.1 | async-start | bytes 524288 | tf_op jit(solution)/shard_map/all_to_all | solution.py:25
  59.9 4.8 %collective-permute-start = (bf16[64,8,256]{2,1,0:T(8,128)(2,1)S(1)}, bf16[64,8,256]{2,1,0:T(8,128)(2,1)S(1)}, u32[]{:S(2)}, u32[]{:S(2)}) collective-permute-start(bf16[64,8,256]{2,1,0:T(8,128)(2,1)S(1)} %all-to-all-done.1), channel_id=1, source_target_pairs={{0,1},{1,0},{2,3},{3,2},{4,5},{5,4},{6,7},{7,6},{8,9},{9,8},{10,11... | collective-permute-start | bytes 786440 | tf_op jit(solution)/shard_map/ppermute | solution.py:84
  63.7 1.2 copy-start.2
  65.0 0.9 copy-start.7
  68.3 3.6 %collective-permute-start.1 = (bf16[64,8,384]{2,1,0:T(8,128)(2,1)S(1)}, bf16[64,8,384]{2,1,0:T(8,128)(2,1)S(1)}, u32[]{:S(2)}, u32[]{:S(2)}) collective-permute-start(bf16[64,8,384]{2,1,0:T(8,128)(2,1)S(1)} %pad_maximum_fusion.2), channel_id=1, source_target_pairs={{0,1},{1,0},{2,3},{3,2},{4,5},{5,4},{6,7},{7,6},{8,9},{9,8},{10,11... | collective-permute-start | bytes 1179656 | tf_op jit(solution)/shard_map/ppermute | solution.py:129
  70.4 7.0 %copy-start.6 = (s32[1,16,16]{2,1,0:T(8,128)S(1)}, s32[1,16,16]{2,1,0:T(8,128)}, u32[]{:S(2)}) copy-start(s32[1,16,16]{2,1,0:T(8,128)} %rows_ref.1) | copy-start | bytes 3076
  72.7 20.5 %all-to-all-start.2 = ((bf16[64,8,384]{2,1,0:T(8,128)(2,1)}), bf16[64,8,384]{2,1,0:T(8,128)(2,1)S(1)}, u32[]{:S(2)}, u32[]{:S(2)}) async-start(bf16[64,8,384]{2,1,0:T(8,128)(2,1)} %add_convert_fusion), calls=%async_computation.2 | async-start | bytes 786432 | tf_op jit(solution)/shard_map/all_to_all | solution.py:25
  94.2 15.3 %all-to-all-start.3 = ((bf16[16,21,256]{2,1,0:T(8,128)(2,1)}), bf16[16,21,256]{2,1,0:T(8,128)(2,1)S(1)}, u32[]{:S(2)}, u32[]{:S(2)}) async-start(bf16[16,21,256]{2,1,0:T(8,128)(2,1)} %pad_maximum_fusion.6), calls=%async_computation.3 | async-start | bytes 393216 | tf_op jit(solution)/shard_map/all_to_all | solution.py:25
  110.3 19.0 %all-to-all-start.4 = ((bf16[64,8,256]{2,1,0:T(8,128)(2,1)}), bf16[64,8,256]{2,1,0:T(8,128)(2,1)S(1)}, u32[]{:S(2)}, u32[]{:S(2)}) async-start(bf16[64,8,256]{2,1,0:T(8,128)(2,1)} %broadcast_in_dim.74), calls=%async_computation.4 | async-start | bytes 524288 | tf_op jit(solution)/shard_map/all_to_all | solution.py:25

commit v5 on v4

--- a/solution.py
+++ b/solution.py
@@ -88,8 +88,8 @@
 
     live = (jnp.arange(slots, dtype=jnp.int32)[None, :] < counts[:, None]).reshape(-1)
     halo_used = jnp.where(live[None, :], halo_weight, jnp.zeros((), BF16))
-    w_both, hub_weight_t = lax.optimization_barrier(
-        (jnp.stack([w_self, w_neigh]), hub_weight.T)
+    w_both, hub_weight_t, grad_out_wide = lax.optimization_barrier(
+        (jnp.stack([w_self, w_neigh]), hub_weight.T, grad_out.astype(F32))
     )
     degree = (
         1.0
@@ -107,7 +107,7 @@
     )
     sig = jax.nn.sigmoid(preact)
     output = (preact * sig).astype(BF16)
-    grad_pre = (grad_out.astype(F32) * (sig + preact * sig * (1.0 - sig))).astype(BF16)
+    grad_pre = (grad_out_wide * (sig + preact * sig * (1.0 - sig))).astype(BF16)
     parts = lax.dot_general(
         jnp.stack([features, neigh]),
         grad_pre,

time: 131 us -> 130 us (level)
  no operation moved by 1% of the time
where the time goes in v5:
time: 130 us
  waiting for transfers between devices  61.9 us (48%)
  starting transfers between devices  51.7 us (40%)
  matrix products  5.15 us (4%)
  other arithmetic  4.33 us (3%)
  local copies, waits for them, and re-layouts  2.84 us (2%)
  Pallas kernels  2.02 us (2%)
  between operations  1.72 us (1%)
    all_to_all x5, waiting for transfers between devices, exchange(): return lax.all_to_all(x, axis, split_axis=0, concat_axis=0, tiled=True)  59.5 us
    all_to_all x5, starting transfers between devices, exchange(): return lax.all_to_all(x, axis, split_axis=0, concat_axis=0, tiled=True)  46.1 us
    ppermute x1, starting transfers between devices, per_device(): other = lax.ppermute(held, 'col', swap)  3.61 us
  transfers between devices with their start and end apart: 7, of which 7 were waited for; matrix products, arithmetic and copies ran while one was open for 4% of the time, Pallas kernels for 0%

profile of v5, /device:TPU:1, one launch (start us, length us, event | category | flops | bytes accessed | tf_op | source)
XLA Modules:
  0.0 129.7 jit_solution(12975616932743149390)
XLA Ops:
  1.3 2.0 %shard_map.129 = bf16[16,18,256]{2,1,0:T(8,128)(2,1)} custom-call(bf16[512,256]{1,0:T(8,128)(2,1)} %features_ref.1, s32[1,16,16]{2,1,0:T(8,128)} %rows_ref.1, s32[1,1]{1,0:T(1,128)} %copy.34.hub_ref, s32[1,16]{1,0:T(1,128)} %count_ref.1), custom_call_target="tpu_custom_call" | custom-call | tf_op jit(solution)/shard_map/pallas_call | solution.py:48
  3.4 17.6 %all-to-all-start = ((bf16[16,18,256]{2,1,0:T(8,128)(2,1)}), bf16[16,18,256]{2,1,0:T(8,128)(2,1)S(1)}, u32[]{:S(2)}, u32[]{:S(2)}) async-start(bf16[16,18,256]{2,1,0:T(8,128)(2,1)} %shard_map.129), calls=%async_computation | async-start | bytes 393216 | tf_op jit(solution)/shard_map/all_to_all | solution.py:25
  21.0 1.4 %convert_reduce_fusion = f32[512]{0:T(512)S(1)} fusion(bf16[512,1024]{1,0:T(8,128)(2,1)} %param.15), kind=kLoop, calls=%fused_computation | loop fusion | flops 1048064 | bytes 1050624 | tf_op jit(solution)/shard_map/reduce_sum | solution.py:97
  22.9 8.4 %all-to-all-done = bf16[16,18,256]{2,1,0:T(8,128)(2,1)S(1)} async-done(((bf16[16,18,256]{2,1,0:T(8,128)(2,1)}), bf16[16,18,256]{2,1,0:T(8,128)(2,1)S(1)}, u32[]{:S(2)}, u32[]{:S(2)}) %all-to-all-start) | async-done | bytes 147488 | tf_op jit(solution)/shard_map/all_to_all | solution.py:25
  31.4 0.7 broadcast_in_dim.67
  32.1 13.9 %all-to-all-start.1 = ((bf16[64,8,256]{2,1,0:T(8,128)(2,1)}), bf16[64,8,256]{2,1,0:T(8,128)(2,1)S(1)}, u32[]{:S(2)}, u32[]{:S(2)}) async-start(bf16[64,8,256]{2,1,0:T(8,128)(2,1)} %broadcast_in_dim.67), calls=%async_computation.1 | async-start | bytes 524288 | tf_op jit(solution)/shard_map/all_to_all | solution.py:25
  46.8 13.0 %all-to-all-done.1 = bf16[64,8,256]{2,1,0:T(8,128)(2,1)S(1)} async-done(((bf16[64,8,256]{2,1,0:T(8,128)(2,1)}), bf16[64,8,256]{2,1,0:T(8,128)(2,1)S(1)}, u32[]{:S(2)}, u32[]{:S(2)}) %all-to-all-start.1) | async-done | bytes 262176 | tf_op jit(solution)/shard_map/all_to_all | solution.py:25
  59.9 3.6 %collective-permute-start = (bf16[64,8,256]{2,1,0:T(8,128)(2,1)S(1)}, bf16[64,8,256]{2,1,0:T(8,128)(2,1)S(1)}, u32[]{:S(2)}, u32[]{:S(2)}) collective-permute-start(bf16[64,8,256]{2,1,0:T(8,128)(2,1)S(1)} %all-to-all-done.1), channel_id=1, source_target_pairs={{0,1},{1,0},{2,3},{3,2},{4,5},{5,4},{6,7},{7,6},{8,9},{9,8},{10,11... | collective-permute-start | bytes 786440 | tf_op jit(solution)/shard_map/ppermute | solution.py:84
  63.8 0.9 collective-permute-done
  65.4 1.1 multiply_convert_fusion
  67.2 0.5 fusion.26
  67.8 2.0 %collective-permute-start.1 = (bf16[64,8,384]{2,1,0:T(8,128)(2,1)S(1)}, bf16[64,8,384]{2,1,0:T(8,128)(2,1)S(1)}, u32[]{:S(2)}, u32[]{:S(2)}) collective-permute-start(bf16[64,8,384]{2,1,0:T(8,128)(2,1)S(1)} %pad_maximum_fusion.2), channel_id=1, source_target_pairs={{0,1},{1,0},{2,3},{3,2},{4,5},{5,4},{6,7},{7,6},{8,9},{9,8},{10,11... | collective-permute-start | bytes 1179656 | tf_op jit(solution)/shard_map/ppermute | solution.py:129
  69.9 1.5 %collective-permute-done.1 = bf16[64,8,384]{2,1,0:T(8,128)(2,1)S(1)} collective-permute-done((bf16[64,8,384]{2,1,0:T(8,128)(2,1)S(1)}, bf16[64,8,384]{2,1,0:T(8,128)(2,1)S(1)}, u32[]{:S(2)}, u32[]{:S(2)}) %collective-permute-start.1) | collective-permute-done | bytes 393248 | tf_op jit(solution)/shard_map/ppermute | solution.py:129
  71.4 0.9 add_convert_fusion
  72.2 4.6 %all-to-all-start.2 = ((bf16[64,8,384]{2,1,0:T(8,128)(2,1)}), bf16[64,8,384]{2,1,0:T(8,128)(2,1)S(1)}, u32[]{:S(2)}, u32[]{:S(2)}) async-start(bf16[64,8,384]{2,1,0:T(8,128)(2,1)} %add_convert_fusion), calls=%async_computation.2 | async-start | bytes 786432 | tf_op jit(solution)/shard_map/all_to_all | solution.py:25
  77.2 15.5 %all-to-all-done.2 = bf16[64,8,384]{2,1,0:T(8,128)(2,1)S(1)} async-done(((bf16[64,8,384]{2,1,0:T(8,128)(2,1)}), bf16[64,8,384]{2,1,0:T(8,128)(2,1)S(1)}, u32[]{:S(2)}, u32[]{:S(2)}) %all-to-all-start.2) | async-done | bytes 393248 | tf_op jit(solution)/shard_map/all_to_all | solution.py:25
  93.0 0.7 pad_maximum_fusion.6
  93.7 4.9 %all-to-all-start.3 = ((bf16[16,21,256]{2,1,0:T(8,128)(2,1)}), bf16[16,21,256]{2,1,0:T(8,128)(2,1)S(1)}, u32[]{:S(2)}, u32[]{:S(2)}) async-start(bf16[16,21,256]{2,1,0:T(8,128)(2,1)} %pad_maximum_fusion.6), calls=%async_computation.3 | async-start | bytes 393216 | tf_op jit(solution)/shard_map/all_to_all | solution.py:25
  99.0 10.0 %all-to-all-done.3 = bf16[16,21,256]{2,1,0:T(8,128)(2,1)S(1)} async-done(((bf16[16,21,256]{2,1,0:T(8,128)(2,1)}), bf16[16,21,256]{2,1,0:T(8,128)(2,1)S(1)}, u32[]{:S(2)}, u32[]{:S(2)}) %all-to-all-start.3) | async-done | bytes 172064 | tf_op jit(solution)/shard_map/all_to_all | solution.py:25
  109.1 0.7 broadcast_in_dim.74
  109.8 5.0 %all-to-all-start.4 = ((bf16[64,8,256]{2,1,0:T(8,128)(2,1)}), bf16[64,8,256]{2,1,0:T(8,128)(2,1)S(1)}, u32[]{:S(2)}, u32[]{:S(2)}) async-start(bf16[64,8,256]{2,1,0:T(8,128)(2,1)} %broadcast_in_dim.74), calls=%async_computation.4 | async-start | bytes 524288 | tf_op jit(solution)/shard_map/all_to_all | solution.py:25
  115.2 1.1 fusion.3
  116.3 12.5 %all-to-all-done.4 = bf16[64,8,256]{2,1,0:T(8,128)(2,1)S(1)} async-done(((bf16[64,8,256]{2,1,0:T(8,128)(2,1)}), bf16[64,8,256]{2,1,0:T(8,128)(2,1)S(1)}, u32[]{:S(2)}, u32[]{:S(2)}) %all-to-all-start.4) | async-done | bytes 262176 | tf_op jit(solution)/shard_map/all_to_all | solution.py:25
  128.9 0.8 slice_bitcast_fusion
  (58 shorter events, 4.4 us)
Async XLA Ops:
  0.6 21.8 %copy-start = (bf16[512,512]{1,0:T(8,128)(2,1)S(1)}, bf16[512,512]{1,0:T(8,128)(2,1)}, u32[]{:S(2)}) copy-start(bf16[512,512]{1,0:T(8,128)(2,1)} %param.13) | copy-start | bytes 1572868
  3.4 19.2 %copy-start.1 = (bf16[512,256]{1,0:T(8,128)(2,1)S(1)}, bf16[512,256]{1,0:T(8,128)(2,1)}, u32[]{:S(2)}) copy-start(bf16[512,256]{1,0:T(8,128)(2,1)} %features_ref.1) | copy-start | bytes 786436
  3.4 28.0 %all-to-all-start = ((bf16[16,18,256]{2,1,0:T(8,128)(2,1)}), bf16[16,18,256]{2,1,0:T(8,128)(2,1)S(1)}, u32[]{:S(2)}, u32[]{:S(2)}) async-start(bf16[16,18,256]{2,1,0:T(8,128)(2,1)} %shard_map.129), calls=%async_computation | async-start | bytes 393216 | tf_op jit(solution)/shard_map/all_to_all | solution.py:25
  22.6 23.4 %copy-start.4 = (bf16[256,256]{1,0:T(8,128)(2,1)S(1)}, bf16[256,256]{1,0:T(8,128)(2,1)}, u32[]{:S(2)}) copy-start(bf16[256,256]{1,0:T(8,128)(2,1)} %param.11) | copy-start | bytes 393220
  22.6 23.4 %copy-start.6 = (bf16[256,256]{1,0:T(8,128)(2,1)S(1)}, bf16[256,256]{1,0:T(8,128)(2,1)}, u32[]{:S(2)}) copy-start(bf16[256,256]{1,0:T(8,128)(2,1)} %param.12) | copy-start | bytes 393220
  22.6 23.5 %copy-start.5 = (bf16[512,256]{1,0:T(8,128)(2,1)S(1)}, bf16[512,256]{1,0:T(8,128)(2,1)}, u32[]{:S(2)}) copy-start(bf16[512,256]{1,0:T(8,128)(2,1)} %param.19) | copy-start | bytes 786436
  31.4 15.3 %copy-start.3 = (bf16[512,256]{1,0:T(8,128)(2,1)S(1)}, bf16[512,256]{1,0:T(8,128)(2,1)}, u32[]{:S(2)}) copy-start(bf16[512,256]{1,0:T(8,128)(2,1)} %param.18) | copy-start | bytes 786436
  32.1 27.8 %all-to-all-start.1 = ((bf16[64,8,256]{2,1,0:T(8,128)(2,1)}), bf16[64,8,256]{2,1,0:T(8,128)(2,1)S(1)}, u32[]{:S(2)}, u32[]{:S(2)}) async-start(bf16[64,8,256]{2,1,0:T(8,128)(2,1)} %broadcast_in_dim.67), calls=%async_computation.1 | async-start | bytes 524288 | tf_op jit(solution)/shard_map/all_to_all | solution.py:25
  59.9 4.8 %collective-permute-start = (bf16[64,8,256]{2,1,0:T(8,128)(2,1)S(1)}, bf16[64,8,256]{2,1,0:T(8,128)(2,1)S(1)}, u32[]{:S(2)}, u32[]{:S(2)}) collective-permute-start(bf16[64,8,256]{2,1,0:T(8,128)(2,1)S(1)} %all-to-all-done.1), channel_id=1, source_target_pairs={{0,1},{1,0},{2,3},{3,2},{4,5},{5,4},{6,7},{7,6},{8,9},{9,8},{10,11... | collective-permute-start | bytes 786440 | tf_op jit(solution)/shard_map/ppermute | solution.py:84
  63.7 1.2 copy-start.2
  67.8 3.6 %collective-permute-start.1 = (bf16[64,8,384]{2,1,0:T(8,128)(2,1)S(1)}, bf16[64,8,384]{2,1,0:T(8,128)(2,1)S(1)}, u32[]{:S(2)}, u32[]{:S(2)}) collective-permute-start(bf16[64,8,384]{2,1,0:T(8,128)(2,1)S(1)} %pad_maximum_fusion.2), channel_id=1, source_target_pairs={{0,1},{1,0},{2,3},{3,2},{4,5},{5,4},{6,7},{7,6},{8,9},{9,8},{10,11... | collective-permute-start | bytes 1179656 | tf_op jit(solution)/shard_map/ppermute | solution.py:129
  69.8 7.0 %copy-start.7 = (s32[1,16,16]{2,1,0:T(8,128)S(1)}, s32[1,16,16]{2,1,0:T(8,128)}, u32[]{:S(2)}) copy-start(s32[1,16,16]{2,1,0:T(8,128)} %rows_ref.1) | copy-start | bytes 3076
  72.2 20.5 %all-to-all-start.2 = ((bf16[64,8,384]{2,1,0:T(8,128)(2,1)}), bf16[64,8,384]{2,1,0:T(8,128)(2,1)S(1)}, u32[]{:S(2)}, u32[]{:S(2)}) async-start(bf16[64,8,384]{2,1,0:T(8,128)(2,1)} %add_convert_fusion), calls=%async_computation.2 | async-start | bytes 786432 | tf_op jit(solution)/shard_map/all_to_all | solution.py:25
  93.7 15.3 %all-to-all-start.3 = ((bf16[16,21,256]{2,1,0:T(8,128)(2,1)}), bf16[16,21,256]{2,1,0:T(8,128)(2,1)S(1)}, u32[]{:S(2)}, u32[]{:S(2)}) async-start(bf16[16,21,256]{2,1,0:T(8,128)(2,1)} %pad_maximum_fusion.6), calls=%async_computation.3 | async-start | bytes 393216 | tf_op jit(solution)/shard_map/all_to_all | solution.py:25
  109.8 19.0 %all-to-all-start.4 = ((bf16[64,8,256]{2,1,0:T(8,128)(2,1)}), bf16[64,8,256]{2,1,0:T(8,128)(2,1)S(1)}, u32[]{:S(2)}, u32[]{:S(2)}) async-start(bf16[64,8,256]{2,1,0:T(8,128)(2,1)} %broadcast_in_dim.74), calls=%async_computation.4 | async-start | bytes 524288 | tf_op jit(solution)/shard_map/all_to_all | solution.py:25
